TPU v7x, 32 devices: a whole 2x2x4 slice. The times are simulated.
32 devices in a mesh: dp: 8 (over z, x), expert: 4 (over y, core).
Axes of the slice: x: 2, y: 2, z: 4, core: 2. Of those that a mesh axis runs over, the one named last changes fastest.
Arguments:
- layer_in: bfloat16 [8192, 1024], P(('dp', 'expert')), may hold values from -6 to 6
- body_of: int32 [8192], P(('dp', 'expert')), may hold values from 0 to 5, as said below
- expert_of: int32 [8192, 1], P(('dp', 'expert')), may hold values from 0 to 7; in each aligned block of 256 rows (0 to 255, 256 to 511, ...) at most 48 rows name the same one
- w_qkv: bfloat16 [1024, 1536], replicated, may hold values from -0.1875 to 0.1875
- w_o: bfloat16 [1024, 512], replicated, may hold values from -0.25 to 0.25
- w_up: bfloat16 [8, 1024, 1024], P('expert', None, 'dp'), may hold values from -0.1875 to 0.1875
- w_down: bfloat16 [8, 1024, 1024], P('expert', 'dp'), may hold values from -0.1875 to 0.1875
- d_out: bfloat16 [8192, 1024], P(('dp', 'expert')), may hold values from -6 to 6
Outputs:
- out: bfloat16 [8192, 1024], P(('dp', 'expert'))
- grad_input: bfloat16 [8192, 1024], P(('dp', 'expert'))
- grad_qkv: float32 [1024, 1536], P(('dp', 'expert'))
- grad_o: float32 [1024, 512], P(('dp', 'expert'))
- grad_up: float32 [8, 1024, 1024], P('expert', None, 'dp')
- grad_down: float32 [8, 1024, 1024], P('expert', 'dp')
Inputs may be any that keep to these rules, and one draw needn't show every extreme that they name: `body_of`: within each device's 256 rows the ids start at 0 and rise by one at each new body; every body has 16 to 128 tokens, no body crosses a multiple of 128 rows of its device, no block of 128 rows holds more than 3 bodies, and some device holds 3 bodies in each of its blocks. `expert_of`: in the 256 rows of one device no expert is named more than 48 times, a bound that some block reaches.
All inputs are finite; a program needn't handle non-finite values.
Results may differ from a plain program's by a relative error of at most 0.014.
Values may be sent and summed in bfloat16 or wider, within the bound.
A program may use at most 128 MiB of HBM per device.

v0:
```python
import jax
import jax.numpy as jnp
from jax import lax
from jax.sharding import PartitionSpec as P

HD = 64


EPSILON = 1e-06


def rms_norm(values):
    scale = lax.rsqrt(jnp.mean(values * values, axis=-1, keepdims=True) + EPSILON)
    return (values * scale).astype(jnp.bfloat16)


def gelu_tanh(values):
    return jax.nn.gelu(values, approximate=True)


def gelu_back(pre_act, cotangent):
    return jax.vjp(gelu_tanh, pre_act)[1](cotangent)[0]


def row_contract(left, right):
    return lax.dot_general(
        left, right, (((0,), (0,)), ((), ())), preferred_element_type=jnp.float32
    )


def col_contract(left, right):
    return lax.dot_general(
        left, right, (((1,), (1,)), ((), ())), preferred_element_type=jnp.float32
    )


def attention_core(packed, labels_row):
    rows = packed.shape[0]
    blocks = rows // 128
    width = packed.shape[1] // 3
    heads = width // HD
    parts = packed.reshape(blocks, 128, 3, heads, HD)
    query = parts[:, :, 0]
    keys = parts[:, :, 1]
    values = parts[:, :, 2]
    scores = jnp.einsum(
        "bqhc,bkhc->bhqk", query, keys, preferred_element_type=jnp.float32
    ) * HD ** (-0.5)
    labels = labels_row.reshape(blocks, 128)
    same = (labels[:, :, None] == labels[:, None, :])[:, None]
    weights = jnp.where(same, jnp.exp(scores), 0.0)
    probs = (weights / jnp.sum(weights, axis=-1, keepdims=True)).astype(jnp.bfloat16)
    mixed = jnp.einsum("bhqk,bkhc->bqhc", probs, values, preferred_element_type=jnp.float32)
    return mixed.astype(jnp.bfloat16).reshape(rows, width)


def on_device(layer_in, body_of, expert_of, w_qkv, w_o, w_up, w_down, d_out):
    tok_rows = layer_in.shape[0]
    width = layer_in.shape[1]
    shards = lax.axis_size("expert")
    local_experts = w_up.shape[0]
    all_experts = local_experts * shards
    capacity = 3 * tok_rows // (2 * all_experts)
    received = shards * capacity
    layer_f = layer_in.astype(jnp.float32)
    normed, norm_x_back = jax.vjp(rms_norm, layer_f)
    packed = jnp.dot(normed, w_qkv, preferred_element_type=jnp.float32).astype(jnp.bfloat16)
    mixed, core_back = jax.vjp(lambda value: attention_core(value, body_of), packed)
    resid = (layer_f + col_contract(mixed, w_o)).astype(jnp.bfloat16)
    inner, norm_h_back = jax.vjp(rms_norm, resid.astype(jnp.float32))
    expert_ids = expert_of[:, 0]
    onehot = (expert_ids[:, None] == jnp.arange(all_experts, dtype=jnp.int32)[None, :]).astype(
        jnp.int32
    )
    ranks = jnp.sum(jnp.cumsum(onehot, axis=0) * onehot, axis=-1) - 1
    slots = expert_ids * capacity + ranks

    def to_slots(values):
        store = jnp.zeros((all_experts * capacity, width), values.dtype).at[slots].set(values)
        return store.reshape(shards, local_experts, capacity, width)

    sent_inner = lax.all_to_all(to_slots(inner), "expert", split_axis=0, concat_axis=2, tiled=True)
    inputs = sent_inner.reshape(local_experts, received, width)
    full_up, full_down = (
        lax.all_gather(w_up, "dp", axis=2, tiled=True),
        lax.all_gather(w_down, "dp", axis=1, tiled=True),
    )
    pre_act = jnp.einsum("esd,edf->esf", inputs, full_up, preferred_element_type=jnp.float32)
    hidden = gelu_tanh(pre_act).astype(jnp.bfloat16)
    result = jnp.einsum("esf,efd->esd", hidden, full_down, preferred_element_type=jnp.float32)
    outgoing = result.astype(jnp.bfloat16).reshape(1, local_experts, received, width)
    returned = lax.all_to_all(outgoing, "expert", split_axis=2, concat_axis=0, tiled=True)
    expert_out = returned.reshape(all_experts * capacity, width)[slots]
    out = (resid.astype(jnp.float32) + expert_out.astype(jnp.float32)).astype(jnp.bfloat16)
    sent_grads = lax.all_to_all(to_slots(d_out), "expert", split_axis=0, concat_axis=2, tiled=True)
    grads_in = sent_grads.reshape(local_experts, received, width)
    d_hidden = jnp.einsum("esd,efd->esf", grads_in, full_down, preferred_element_type=jnp.float32)
    d_pre = gelu_back(pre_act, d_hidden).astype(jnp.bfloat16)
    part_up = jnp.einsum("esd,esf->edf", inputs, d_pre, preferred_element_type=jnp.float32)
    part_down = jnp.einsum("esf,esd->efd", hidden, grads_in, preferred_element_type=jnp.float32)
    d_inputs = jnp.einsum("esf,edf->esd", d_pre, full_up, preferred_element_type=jnp.float32)
    going_back = d_inputs.astype(jnp.bfloat16).reshape(1, local_experts, received, width)
    came_back = lax.all_to_all(going_back, "expert", split_axis=2, concat_axis=0, tiled=True)
    d_inner = came_back.reshape(all_experts * capacity, width)[slots]
    grad_up, grad_down = (
        lax.psum_scatter(
            part_up.astype(jnp.bfloat16), "dp", scatter_dimension=2, tiled=True
        ).astype(jnp.float32),
        lax.psum_scatter(
            part_down.astype(jnp.bfloat16), "dp", scatter_dimension=1, tiled=True
        ).astype(jnp.float32),
    )
    d_resid = (d_out.astype(jnp.float32) + norm_h_back(d_inner)[0]).astype(jnp.bfloat16)
    term_o = row_contract(d_resid, mixed)
    d_mixed = jnp.dot(d_resid, w_o, preferred_element_type=jnp.float32).astype(jnp.bfloat16)
    d_packed = core_back(d_mixed)[0]
    term_qkv = row_contract(normed, d_packed)
    grad_qkv, grad_o = (
        lax.psum_scatter(term_qkv, ("dp", "expert"), scatter_dimension=0, tiled=True),
        lax.psum_scatter(term_o, ("dp", "expert"), scatter_dimension=0, tiled=True),
    )
    d_normed = col_contract(d_packed, w_qkv).astype(jnp.bfloat16)
    grad_input = (d_resid.astype(jnp.float32) + norm_x_back(d_normed)[0]).astype(jnp.bfloat16)
    return (out, grad_input, grad_qkv, grad_o, grad_up, grad_down)


def solution(mesh):
    in_specs = (
        P(("dp", "expert"), None),
        P(("dp", "expert")),
        P(("dp", "expert"), None),
        P(),
        P(),
        P("expert", None, "dp"),
        P("expert", "dp", None),
        P(("dp", "expert"), None),
    )
    out_specs = (
        P(("dp", "expert"), None),
        P(("dp", "expert"), None),
        P(("dp", "expert"), None),
        P(("dp", "expert"), None),
        P("expert", None, "dp"),
        P("expert", "dp", None),
    )
    return jax.shard_map(
        on_device, mesh=mesh, in_specs=in_specs, out_specs=out_specs, check_vma=False
    )
```

profile of v0, /device:TPU:0, one launch (start us, length us, event | category | flops | bytes accessed | tf_op | source)
XLA Modules:
  0.0 630.3 jit_solution(3287069089571837965)
XLA Ops:
  14.7 4.2 all-to-all-start.2
  42.3 4.2 all-to-all-start
  48.9 9.9 %all-to-all-done = bf16[4,2,48,1024]{3,2,1,0:T(8,128)(2,1)} async-done(((bf16[4,2,48,1024]{3,2,1,0:T(8,128)(2,1)}), bf16[4,2,48,1024]{3,2,1,0:T(8,128)(2,1)}, u32[]{:S(2)}, u32[]{:S(2)}) %all-to-all-start) | async-done | bytes 786464 | tf_op jit(solution)/shard_map/all_to_all | solution.py:82
  60.9 25.4 %all-gather.5.cloned.1.call-done = bf16[2,1024,1024]{2,1,0:T(8,128)(2,1)} async-done(((bf16[2,128,1024]{2,1,0:T(8,128)(2,1)}), bf16[2,1024,1024]{2,1,0:T(8,128)(2,1)}) %all-gather.5.cloned.1.call-update) | async-done | bytes 4194320 | tf_op jit(solution)/shard_map/all_gather | solution.py:86
  86.3 5.1 fusion.65
  91.4 70.3 %all-gather.3.cloned.1.call-done = bf16[2,1024,1024]{2,1,0:T(8,128)(2,1)} async-done(((bf16[2,1024,128]{2,1,0:T(8,128)(2,1)}), bf16[2,1024,1024]{2,1,0:T(8,128)(2,1)}) %all-gather.3.cloned.1.call-update) | async-done | bytes 4194320 | tf_op jit(solution)/shard_map/all_gather | solution.py:85
  161.7 6.0 fusion.6
  168.5 3.2 convolution_convert_fusion.1
  171.7 11.3 %copy.64 = bf16[2,1024,1024]{1,0,2:T(2,128)(2,1)} copy(bf16[2,1024,1024]{2,1,0:T(8,128)(2,1)} %convolution_convert_fusion.1) | data formatting | bytes 8388608
  183.1 5.6 copy.73
  188.7 4.9 convolution_convert_fusion
  193.6 4.1 fusion.9
  199.4 4.2 all-to-all-start.3
  203.6 3.9 fusion.8
  209.2 6.1 all-to-all-done.3
  215.3 4.2 all-to-all-start.1
  222.0 9.2 %all-to-all-done.1 = bf16[1,2,192,1024]{3,1,0,2:T(2,128)(2,1)} async-done(((bf16[1,2,192,1024]{3,1,0,2:T(2,128)(2,1)}), bf16[1,2,192,1024]{3,1,0,2:T(2,128)(2,1)}, u32[]{:S(2)}, u32[]{:S(2)}) %all-to-all-start.1) | async-done | bytes 786464 | tf_op jit(solution)/shard_map/all_to_all | solution.py:92
  233.5 3.6 gather_fusion.1
  237.1 3.6 gather_fusion
  259.6 3.8 fusion.32
  267.1 7.8 %reduce-scatter.13.cloned.1.call-done = bf16[128,2048]{1,0:T(8,128)(2,1)} async-done(((bf16[1024,2048]{1,0:T(8,128)(2,1)}), bf16[128,2048]{1,0:T(8,128)(2,1)}) %reduce-scatter.13.cloned.1.call-update) | async-done | bytes 524304
  281.2 85.5 %reduce-scatter.11.cloned.1.call-done = bf16[2,128,1024]{2,1,0:T(8,128)(2,1)} async-done(((bf16[2,1024,1024]{2,1,0:T(8,128)(2,1)}), bf16[2,128,1024]{2,1,0:T(8,128)(2,1)}) %reduce-scatter.11.cloned.1.call-update) | async-done | bytes 524304 | tf_op jit(solution)/shard_map/reduce_scatter | solution.py:109
  368.8 137.2 %reduce-scatter.9.cloned.1.call-done = f32[32,512]{1,0:T(8,128)} async-done(((f32[1024,512]{1,0:T(8,128)}), f32[32,512]{1,0:T(8,128)}) %reduce-scatter.9.cloned.1.call-update) | async-done | bytes 65552 | tf_op jit(solution)/shard_map/reduce_scatter | solution.py:120
  506.0 117.4 %reduce-scatter.7.cloned.1.call-done = f32[32,1536]{1,0:T(8,128)} async-done(((f32[1024,1536]{1,0:T(8,128)}), f32[32,1536]{1,0:T(8,128)}) %reduce-scatter.7.cloned.1.call-update) | async-done | bytes 196624 | tf_op jit(solution)/shard_map/reduce_scatter | solution.py:119
  (107 shorter events, 75.2 us)
Async XLA Ops:
  7.2 13.1 %copy-start = (bf16[1024,1536]{1,0:T(8,128)(2,1)S(1)}, bf16[1024,1536]{1,0:T(8,128)(2,1)}, u32[]{:S(2)}) copy-start(bf16[1024,1536]{1,0:T(8,128)(2,1)} %param.11) | copy-start | bytes 9437188
  7.2 79.1 %all-gather.5.cloned.1.call-start = ((), (), s32[]{:S(2)}) async-start(), calls=%async_computation.9 | async-start | bytes 4718592 | tf_op jit(solution)/shard_map/all_gather | solution.py:86
  7.9 153.8 %all-gather.3.cloned.1.call-start = ((), (), s32[]{:S(2)}) async-start(), calls=%async_computation.8 | async-start | bytes 4718592 | tf_op jit(solution)/shard_map/all_gather | solution.py:85
  14.7 27.6 %all-to-all-start.2 = ((bf16[4,2,48,1024]{3,2,1,0:T(8,128)(2,1)}), bf16[4,2,48,1024]{3,2,1,0:T(8,128)(2,1)}, u32[]{:S(2)}, u32[]{:S(2)}) async-start(bf16[4,2,48,1024]{3,2,1,0:T(8,128)(2,1)} %bitcast.121), calls=%async_computation.2 | async-start | bytes 1572864 | tf_op jit(solution)/shard_map/all_to_all | solution.py:95
  28.9 5.4 copy-start.19
  35.8 1.5 copy-start.3
  35.9 1.9 copy-start.14
  37.4 1.7 copy-start.15
  42.3 16.5 %all-to-all-start = ((bf16[4,2,48,1024]{3,2,1,0:T(8,128)(2,1)}), bf16[4,2,48,1024]{3,2,1,0:T(8,128)(2,1)}, u32[]{:S(2)}, u32[]{:S(2)}) async-start(bf16[4,2,48,1024]{3,2,1,0:T(8,128)(2,1)} %bitcast.122), calls=%async_computation | async-start | bytes 1572864 | tf_op jit(solution)/shard_map/all_to_all | solution.py:82
  46.5 228.4 %reduce-scatter.13.cloned.1.call-start = ((), (), s32[]{:S(2)}) async-start(), calls=%async_computation.13 | async-start | bytes 4718592
  161.7 6.8 %copy-start.10 = (bf16[1,2,4,48,1024]{4,3,2,1,0:T(8,128)(2,1)S(1)}, bf16[1,2,4,48,1024]{4,3,2,1,0:T(8,128)(2,1)}, u32[]{:S(2)}) copy-start(bf16[1,2,4,48,1024]{4,3,2,1,0:T(8,128)(2,1)} %copy.47) | copy-start | bytes 2359300
  188.6 178.1 %reduce-scatter.11.cloned.1.call-start = ((), (), s32[]{:S(2)}) async-start(), calls=%async_computation.12 | async-start | bytes 4718592 | tf_op jit(solution)/shard_map/reduce_scatter | solution.py:109
  199.4 15.9 %all-to-all-start.3 = ((bf16[1,2,192,1024]{3,1,0,2:T(2,128)(2,1)}), bf16[1,2,192,1024]{3,1,0,2:T(2,128)(2,1)}, u32[]{:S(2)}, u32[]{:S(2)}) async-start(bf16[1,2,192,1024]{3,1,0,2:T(2,128)(2,1)} %copy.51), calls=%async_computation.3 | async-start | bytes 1572864 | tf_op jit(solution)/shard_map/all_to_all | solution.py:103
  215.3 15.9 %all-to-all-start.1 = ((bf16[1,2,192,1024]{3,1,0,2:T(2,128)(2,1)}), bf16[1,2,192,1024]{3,1,0,2:T(2,128)(2,1)}, u32[]{:S(2)}, u32[]{:S(2)}) async-start(bf16[1,2,192,1024]{3,1,0,2:T(2,128)(2,1)} %copy.48), calls=%async_computation.1 | async-start | bytes 1572864 | tf_op jit(solution)/shard_map/all_to_all | solution.py:92
  219.5 286.5 %reduce-scatter.9.cloned.1.call-start = ((), (), s32[]{:S(2)}) async-start(), calls=%async_computation.11 | async-start | bytes 2162688 | tf_op jit(solution)/shard_map/reduce_scatter | solution.py:120
  242.1 3.6 copy-start.16
  247.6 375.9 %reduce-scatter.7.cloned.1.call-start = ((), (), s32[]{:S(2)}) async-start(), calls=%async_computation.10 | async-start | bytes 6488064 | tf_op jit(solution)/shard_map/reduce_scatter | solution.py:119
  253.7 2.2 copy-start.7
  253.7 2.2 copy-start.13
  253.7 2.7 copy-start.9
  253.7 2.7 copy-start.17
  257.8 1.8 copy-start.4
  263.4 2.5 copy-start.2
  263.4 2.5 copy-start.5
  (6 other events, 5.8 us)
Sparse Core Ops, SparseCore 0:
  10.2 76.0 all-gather.4
  88.3 73.2 all-gather.2
  188.8 86.0 reduce-scatter.12
  278.8 87.8 reduce-scatter.10
  369.4 136.5 reduce-scatter.8
  513.0 110.3 reduce-scatter.6
where the time goes:
time: 632 us; the launch traced here: 630 us
  waiting for transfers between devices  470 us (74%)
  local copies, waits for them, and re-layouts  63.7 us (10%)
  matrix products  47.3 us (7%)
  starting transfers between devices  17.5 us (3%)
  other arithmetic  17.1 us (3%)
  between operations  14.5 us (2%)
    reduce_scatter x1, waiting for transfers between devices, on_device(): lax.psum_scatter(term_o, ('dp', 'expert'), scatter_dimension=0, tiled=True)  137 us
    reduce_scatter x1, waiting for transfers between devices, on_device(): lax.psum_scatter(term_qkv, ('dp', 'expert'), scatter_dimension=0, tiled=T...  117 us
    reduce_scatter x1, waiting for transfers between devices, on_device(): lax.psum_scatter(part_down.astype(jnp.bfloat16), 'dp', scatter_dimension=...  85.5 us
    all_gather x1, waiting for transfers between devices, on_device(): lax.all_gather(w_up, 'dp', axis=2, tiled=True)  70.3 us
    unnamed x47, local copies, waits for them, and re-layouts  30.8 us
    all_gather x1, waiting for transfers between devices, on_device(): lax.all_gather(w_down, 'dp', axis=1, tiled=True)  25.4 us
  transfers between devices with their start and end apart: 10, of which 9 were waited for; matrix products, arithmetic and copies ran while one was open for 16% of the time, Pallas kernels for 0%

commit v1 on v0

v1 whole, which is shorter than its diff:
```python
import jax
import jax.numpy as jnp
from jax import lax
from jax.sharding import PartitionSpec as P

HD = 64


EPSILON = 1e-06


def rms_norm(values):
    scale = lax.rsqrt(jnp.mean(values * values, axis=-1, keepdims=True) + EPSILON)
    return (values * scale).astype(jnp.bfloat16)


def gelu_tanh(values):
    return jax.nn.gelu(values, approximate=True)


def gelu_back(pre_act, cotangent):
    return jax.vjp(gelu_tanh, pre_act)[1](cotangent)[0]


def row_contract(left, right):
    return lax.dot_general(
        left, right, (((0,), (0,)), ((), ())), preferred_element_type=jnp.float32
    )


def col_contract(left, right):
    return lax.dot_general(
        left, right, (((1,), (1,)), ((), ())), preferred_element_type=jnp.float32
    )


def attention_core(packed, labels_row):
    rows = packed.shape[0]
    blocks = rows // 128
    width = packed.shape[1] // 3
    heads = width // HD
    parts = packed.reshape(blocks, 128, 3, heads, HD)
    query = parts[:, :, 0]
    keys = parts[:, :, 1]
    values = parts[:, :, 2]
    scores = jnp.einsum(
        "bqhc,bkhc->bhqk", query, keys, preferred_element_type=jnp.float32
    ) * HD ** (-0.5)
    labels = labels_row.reshape(blocks, 128)
    same = (labels[:, :, None] == labels[:, None, :])[:, None]
    weights = jnp.where(same, jnp.exp(scores), 0.0)
    probs = (weights / jnp.sum(weights, axis=-1, keepdims=True)).astype(jnp.bfloat16)
    mixed = jnp.einsum("bhqk,bkhc->bqhc", probs, values, preferred_element_type=jnp.float32)
    return mixed.astype(jnp.bfloat16).reshape(rows, width)


def stage_perm(count, bit):
    return [(i, i ^ bit) for i in range(count)]


def halve(values, axis_name, count, axis, bit):
    own = (lax.axis_index(axis_name) // bit) % 2
    keep = lax.dynamic_index_in_dim(values, own, axis, keepdims=False)
    give = lax.dynamic_index_in_dim(values, 1 - own, axis, keepdims=False).astype(jnp.bfloat16)
    came = lax.ppermute(give, axis_name, stage_perm(count, bit))
    return keep + came.astype(jnp.float32)


def scatter_sum(term):
    groups, shards = lax.axis_size("dp"), lax.axis_size("expert")
    rows, cols = term.shape
    own_rows = rows // (groups * shards)
    left = shards
    value = term.reshape(groups * shards * own_rows, cols)
    lead = groups
    bit = 1
    while bit < shards:
        left //= 2
        value = halve(value.reshape(lead, left, 2, own_rows, cols), "expert", shards, 2, bit)
        bit *= 2
    left = groups
    bit = 1
    while bit < groups:
        left //= 2
        value = halve(value.reshape(left, 2, own_rows, cols), "dp", groups, 1, bit)
        bit *= 2
    return value.reshape(own_rows, cols)


def ring_pairs(groups, step):
    half = groups // 2
    return [(i, ((i // 2 + step) % half) * 2 + i % 2) for i in range(groups)]


def ring_gather(shard, pairs, count):
    slots = [shard]
    for _ in range(count - 1):
        slots.append(lax.ppermute(slots[-1], "dp", pairs))
    return slots


def ring_reduce(slots, pairs):
    count = len(slots)
    total = slots[1 % count]
    for step in range(count - 1):
        came = lax.ppermute(total.astype(jnp.bfloat16), "dp", pairs)
        total = came.astype(jnp.float32) + slots[(step + 2) % count]
    return total


def on_device(layer_in, body_of, expert_of, w_qkv, w_o, w_up, w_down, d_out):
    tok_rows = layer_in.shape[0]
    width = layer_in.shape[1]
    shards = lax.axis_size("expert")
    groups = lax.axis_size("dp")
    half = groups // 2
    local_experts = w_up.shape[0]
    all_experts = local_experts * shards
    capacity = 3 * tok_rows // (2 * all_experts)
    received = shards * capacity
    partner = stage_perm(groups, 1)
    forth, back = ring_pairs(groups, 1), ring_pairs(groups, -1)

    full_up = jnp.concatenate(ring_gather(w_up, forth, half), axis=2)
    full_down = jnp.concatenate(ring_gather(w_down, forth, half), axis=1)

    ids = expert_of[:, 0]
    at = jnp.arange(tok_rows, dtype=jnp.int32)
    earlier = (ids[:, None] == ids[None, :]) & (at[None, :] < at[:, None])
    ranks = jnp.sum(earlier.astype(jnp.int32), axis=1)
    slots = ids * capacity + ranks
    places = jnp.arange(all_experts * capacity, dtype=jnp.int32)
    spread = (places[:, None] == slots[None, :]).astype(jnp.bfloat16)

    def to_experts(values):
        store = jnp.dot(spread, values, preferred_element_type=jnp.float32).astype(jnp.bfloat16)
        store = store.reshape(shards, local_experts, capacity, width)
        sent = lax.all_to_all(store, "expert", split_axis=0, concat_axis=2, tiled=True)
        own = sent.reshape(local_experts, received, width)
        return jnp.concatenate([own, lax.ppermute(own, "dp", partner)], axis=1)

    def to_tokens(values):
        other = lax.ppermute(values[:, received:].astype(jnp.bfloat16), "dp", partner)
        total = (values[:, :received] + other.astype(jnp.float32)).astype(jnp.bfloat16)
        total = total.reshape(local_experts, shards, capacity, width)
        returned = lax.all_to_all(total, "expert", split_axis=1, concat_axis=0, tiled=True)
        returned = returned.reshape(all_experts * capacity, width)
        return row_contract(spread, returned)

    grads_in = to_experts(d_out)
    layer_f = layer_in.astype(jnp.float32)
    normed, norm_x_back = jax.vjp(rms_norm, layer_f)
    packed = jnp.dot(normed, w_qkv, preferred_element_type=jnp.float32).astype(jnp.bfloat16)
    mixed, core_back = jax.vjp(lambda value: attention_core(value, body_of), packed)
    resid = (layer_f + col_contract(mixed, w_o)).astype(jnp.bfloat16)
    inner, norm_h_back = jax.vjp(rms_norm, resid.astype(jnp.float32))
    inputs = to_experts(inner)
    d_hidden = jnp.einsum("esd,efd->esf", grads_in, full_down, preferred_element_type=jnp.float32)
    pre_act = jnp.einsum("esd,edf->esf", inputs, full_up, preferred_element_type=jnp.float32)
    hidden = gelu_tanh(pre_act).astype(jnp.bfloat16)
    d_pre = gelu_back(pre_act, d_hidden).astype(jnp.bfloat16)
    d_inputs = jnp.einsum("esf,edf->esd", d_pre, full_up, preferred_element_type=jnp.float32)
    d_inner = to_tokens(d_inputs).astype(jnp.bfloat16)
    part_up = jnp.einsum("esd,esf->edf", inputs, d_pre, preferred_element_type=jnp.float32)
    part_down = jnp.einsum("esf,esd->efd", hidden, grads_in, preferred_element_type=jnp.float32)
    grad_up = ring_reduce(jnp.split(part_up, half, axis=2), forth)
    grad_down = ring_reduce(jnp.split(part_down, half, axis=1), forth)
    result = jnp.einsum("esf,efd->esd", hidden, full_down, preferred_element_type=jnp.float32)
    expert_out = to_tokens(result)
    out = (resid.astype(jnp.float32) + expert_out).astype(jnp.bfloat16)
    d_resid = (d_out.astype(jnp.float32) + norm_h_back(d_inner)[0]).astype(jnp.bfloat16)
    grad_o = scatter_sum(row_contract(d_resid, mixed))
    d_mixed = jnp.dot(d_resid, w_o, preferred_element_type=jnp.float32).astype(jnp.bfloat16)
    d_packed = core_back(d_mixed)[0]
    grad_qkv = scatter_sum(row_contract(normed, d_packed))
    d_normed = col_contract(d_packed, w_qkv).astype(jnp.bfloat16)
    grad_input = (d_resid.astype(jnp.float32) + norm_x_back(d_normed)[0]).astype(jnp.bfloat16)
    return (out, grad_input, grad_qkv, grad_o, grad_up, grad_down)


def solution(mesh):
    in_specs = (
        P(("dp", "expert"), None),
        P(("dp", "expert")),
        P(("dp", "expert"), None),
        P(),
        P(),
        P("expert", None, "dp"),
        P("expert", "dp", None),
        P(("dp", "expert"), None),
    )
    out_specs = (
        P(("dp", "expert"), None),
        P(("dp", "expert"), None),
        P(("dp", "expert"), None),
        P(("dp", "expert"), None),
        P("expert", None, "dp"),
        P("expert", "dp", None),
    )
    return jax.shard_map(
        on_device, mesh=mesh, in_specs=in_specs, out_specs=out_specs, check_vma=False
    )
```

time: 632 us -> 251 us (0.40)
  waiting for transfers between devices: 470 us -> 73.1 us
  starting transfers between devices: 17.5 us -> 46.4 us
  between operations: 14.5 us -> 1.29 us
  other arithmetic: 17.1 us -> 28.9 us
  matrix products: 47.3 us -> 40.9 us
    reduce_scatter x3 -> x0, waiting for transfers between devices: 340 us -> none  [the longest x1 137 us: on_device(): lax.psum_scatter(term_o, ('dp', 'expert'), scatter_dimension=0, tiled=True)]
    all_gather x2 -> x0, waiting for transfers between devices: 95.6 us -> none  [the longest x1 70.3 us: on_device(): lax.all_gather(w_up, 'dp', axis=2, tiled=True)]
    ppermute x0 -> x26, waiting for transfers between devices: none -> 63.7 us  [the longest x10 32.1 us: halve(): came = lax.ppermute(give, axis_name, stage_perm(count, bit))]
    ppermute x0 -> x26, starting transfers between devices: none -> 29.6 us  [the longest x10 11.6 us: halve(): came = lax.ppermute(give, axis_name, stage_perm(count, bit))]
    all_to_all x4, waiting for transfers between devices: 25.2 us -> 9.44 us  [the longest x2 7.66 us: to_experts(): lax.all_to_all(store, 'expert', split_axis=0, concat_axis=2, tiled=True)]
    add x0 -> x11, other arithmetic: none -> 10.3 us  [the longest x2 4.95 us: ring_reduce(): total = came.astype(jnp.float32) + slots[(step + 2) % count]]
    unnamed x7 -> x0, waiting for transfers between devices: 9.28 us -> none
    gather x2 -> x0, local copies, waits for them, and re-layouts: 7.18 us -> none  [the longest x1 3.59 us: on_device(): expert_out = returned.reshape(all_experts * capacity, width)[slots]]
  transfers between devices with their start and end apart: 10 -> 30, of which waited for: 9 -> 13; matrix products, arithmetic and copies ran while one was open for 16% -> 43% of each run, Pallas kernels for 0% -> 0%
where the time goes in v1:
time: 251 us; the launch traced here: 248 us
  waiting for transfers between devices  73.1 us (29%)
  local copies, waits for them, and re-layouts  57.9 us (23%)
  starting transfers between devices  46.4 us (18%)
  matrix products  40.9 us (16%)
  other arithmetic  28.9 us (12%)
    ppermute x10, waiting for transfers between devices, halve(): came = lax.ppermute(give, axis_name, stage_perm(count, bit))  32.1 us
    unnamed x79, local copies, waits for them, and re-layouts  28.1 us
    ppermute x6, waiting for transfers between devices, ring_gather(): slots.append(lax.ppermute(slots[-1], 'dp', pairs))  14 us
    ppermute x10, starting transfers between devices, halve(): came = lax.ppermute(give, axis_name, stage_perm(count, bit))  11.6 us
    ppermute x2, waiting for transfers between devices, to_tokens(): lax.ppermute(values[:, received:].astype(jnp.bfloat16), 'dp', partner)  9.45 us
    convert_element_type x4, other arithmetic, ring_reduce(): came = lax.ppermute(total.astype(jnp.bfloat16), 'dp', pairs)  9.36 us
    all_to_all x2, starting transfers between devices, to_experts(): lax.all_to_all(store, 'expert', split_axis=0, concat_axis=2, tiled=True)  8.4 us
    all_to_all x2, starting transfers between devices, to_tokens(): lax.all_to_all(total, 'expert', split_axis=1, concat_axis=0, tiled=True)  8.38 us
  transfers between devices with their start and end apart: 30, of which 13 were waited for; matrix products, arithmetic and copies ran while one was open for 43% of the time, Pallas kernels for 0%

profile of v1, /device:TPU:0, one launch (start us, length us, event | category | flops | bytes accessed | tf_op | source)
XLA Modules:
  0.0 248.4 jit_solution(4098963044247727574)
XLA Ops:
  0.6 3.1 %collective-permute-start.1 = (bf16[2,1024,128]{2,1,0:T(8,128)(2,1)}, bf16[2,1024,128]{2,1,0:T(8,128)(2,1)}, u32[]{:S(2)}, u32[]{:S(2)}) collective-permute-start(bf16[2,1024,128]{2,1,0:T(8,128)(2,1)} %param.13), channel_id=1, source_target_pairs={{0,8},{4,12},{8,16},{12,20},{16,24},{20,28},{24,0},{28,4},{1,9},{5... | collective-permute-start | bytes 1572872 | tf_op jit(solution)/shard_map/ppermute | solution.py:98
  9.0 3.0 %convolution_convert_fusion = bf16[256,1536]{1,0:T(8,128)(2,1)} fusion(bf16[1024,1536]{1,0:T(8,128)(2,1)S(1)} %copy-done, bf16[256,1024]{1,0:T(8,128)(2,1)} %param.8, f32[256]{0:T(256)S(1)} %fusion.71), kind=kOutput, calls=%fused_computation.2 | convolution fusion | flops 806486016 | bytes 4457472 | tf_op jit(solution)/shard_map/dot_general | solution.py:153
  12.0 3.1 %reshape.185 = bf16[2,128,3,8,64]{4,3,2,1,0:T(8,128)(2,1)} reshape(bf16[256,1536]{1,0:T(8,128)(2,1)} %convolution_convert_fusion) | data formatting | bytes 1572864 | tf_op jit(solution)/shard_map/jvp()/reshape | solution.py:42
  29.1 4.2 %all-to-all-start = ((bf16[4,2,48,1024]{3,2,1,0:T(8,128)(2,1)}), bf16[4,2,48,1024]{3,2,1,0:T(8,128)(2,1)}, u32[]{:S(2)}, u32[]{:S(2)}) async-start(bf16[4,2,48,1024]{3,2,1,0:T(8,128)(2,1)} %bitcast.159), calls=%async_computation | async-start | bytes 1572864 | tf_op jit(solution)/shard_map/all_to_all | solution.py:138
  37.4 7.7 %all-to-all-done = bf16[4,2,48,1024]{3,2,1,0:T(8,128)(2,1)} async-done(((bf16[4,2,48,1024]{3,2,1,0:T(8,128)(2,1)}), bf16[4,2,48,1024]{3,2,1,0:T(8,128)(2,1)}, u32[]{:S(2)}, u32[]{:S(2)}) %all-to-all-start) | async-done | bytes 786464 | tf_op jit(solution)/shard_map/all_to_all | solution.py:138
  45.1 4.2 %all-to-all-start.2 = ((bf16[4,2,48,1024]{3,2,1,0:T(8,128)(2,1)}), bf16[4,2,48,1024]{3,2,1,0:T(8,128)(2,1)}, u32[]{:S(2)}, u32[]{:S(2)}) async-start(bf16[4,2,48,1024]{3,2,1,0:T(8,128)(2,1)} %bitcast.158), calls=%async_computation.2 | async-start | bytes 1572864 | tf_op jit(solution)/shard_map/all_to_all | solution.py:138
  57.2 4.3 %collective-permute-done.5 = bf16[2,128,1024]{2,1,0:T(8,128)(2,1)} collective-permute-done((bf16[2,128,1024]{2,1,0:T(8,128)(2,1)}, bf16[2,128,1024]{2,1,0:T(8,128)(2,1)}, u32[]{:S(2)}, u32[]{:S(2)}) %collective-permute-start.5) | collective-permute-done | bytes 524320 | tf_op jit(solution)/shard_map/ppermute | solution.py:98
  74.6 8.8 %collective-permute-done.6 = bf16[2,128,1024]{2,1,0:T(8,128)(2,1)} collective-permute-done((bf16[2,128,1024]{2,1,0:T(8,128)(2,1)}, bf16[2,128,1024]{2,1,0:T(8,128)(2,1)}, u32[]{:S(2)}, u32[]{:S(2)}) %collective-permute-start.6) | collective-permute-done | bytes 524320 | tf_op jit(solution)/shard_map/ppermute | solution.py:98
  85.4 3.0 %fusion.40 = f32[2,384,512]{2,1,0:T(8,128)S(1)} fusion(bf16[2,1024,512]{2,1,0:T(8,128)(2,1)} %constant_dynamic-update-slice_fusion, bf16[2,192,1024]{2,1,0:T(8,128)(2,1)} %collective-permute-done, bf16[2,192,1024]{2,1,0:T(8,128)(2,1)} %bitcast.9), kind=kOutput, calls=%fused_computation.92 | convolution fusion | flops 808452096 | bytes 5242880 | tf_op jit(solution)/shard_map/esd,edf->esf/dot_general | solution.py:159
  90.3 3.7 %fusion.6 = bf16[2,384,512]{2,1,0:T(8,128)(2,1)S(1)} fusion(f32[2,384,512]{2,1,0:T(8,128)S(1)} %fusion.40, bf16[2,512,1024]{2,1,0:T(8,128)(2,1)} %constant_dynamic-update-slice_fusion.4, bf16[2,192,1024]{2,1,0:T(8,128)(2,1)S(1)} %collective-permute-done.8, bf16[2,192,1024]{2,1,0:T(8,128)(2,1)S(1)} %bitcast.175), kind=kOutput, calls=%fused_computation.21 | convolution fusion | flops 816316416 | bytes 6029312 | tf_op jit(solution)/shard_map/esd,efd->esf/dot_general | solution.py:158
  94.0 2.9 %fusion.81 = f32[2,384,1024]{2,1,0:T(8,128)S(1)} fusion(bf16[2,384,512]{2,1,0:T(8,128)(2,1)S(1)} %fusion.6, bf16[2,1024,512]{2,1,0:T(8,128)(2,1)} %constant_dynamic-update-slice_fusion), kind=kOutput, calls=%fused_computation.165 | convolution fusion | flops 805306368 | bytes 6029312 | tf_op jit(solution)/shard_map/esf,edf->esd/dot_general | solution.py:162
  101.1 3.3 %fusion.79 = f32[2,384,1024]{2,1,0:T(8,128)S(1)} fusion(bf16[2,512,1024]{2,1,0:T(8,128)(2,1)} %constant_dynamic-update-slice_fusion.4, f32[2,384,512]{2,1,0:T(8,128)} %copy-done.22), kind=kOutput, calls=%fused_computation.163 | convolution fusion | flops 808845312 | bytes 6815744 | tf_op jit(solution)/shard_map/esf,efd->esd/dot_general | solution.py:168
  110.9 9.4 %collective-permute-done.9 = bf16[2,192,1024]{2,1,0:T(8,128)(2,1)} collective-permute-done((bf16[2,192,1024]{2,1,0:T(8,128)(2,1)}, bf16[2,192,1024]{2,1,0:T(8,128)(2,1)}, u32[]{:S(2)}, u32[]{:S(2)}) %collective-permute-start.9) | collective-permute-done | bytes 786464 | tf_op jit(solution)/shard_map/ppermute | solution.py:143
  122.7 4.2 %all-to-all-start.3 = ((bf16[2,4,48,1024]{3,2,0,1:T(8,128)(2,1)}), bf16[2,4,48,1024]{3,2,0,1:T(8,128)(2,1)}, u32[]{:S(2)}, u32[]{:S(2)}) async-start(bf16[2,4,48,1024]{3,2,0,1:T(8,128)(2,1)} %copy.62), calls=%async_computation.3 | async-start | bytes 1572864 | tf_op jit(solution)/shard_map/all_to_all | solution.py:146
  126.9 2.9 %fusion.39 = f32[2,1024,512]{2,1,0:T(8,128)S(1)} fusion(bf16[2,384,512]{2,1,0:T(8,128)(2,1)} %copy-done.18, bf16[2,192,1024]{2,1,0:T(8,128)(2,1)} %collective-permute-done, bf16[2,192,1024]{2,1,0:T(8,128)(2,1)} %bitcast.9), kind=kOutput, calls=%fused_computation.91 | convolution fusion | flops 808452096 | bytes 6553600 | tf_op jit(solution)/shard_map/esd,esf->edf/dot_general | solution.py:164
  159.3 2.7 %copy-done.1 = f32[8,2,2,32,1536]{4,3,2,1,0:T(8,128)} copy-done((f32[8,2,2,32,1536]{4,3,2,1,0:T(8,128)}, f32[8,2,2,32,1536]{4,3,2,1,0:T(8,128)S(1)}, u32[]{:S(2)}) %copy-start.1) | copy-done | bytes 6291480
  169.8 4.2 %all-to-all-start.1 = ((bf16[2,4,48,1024]{3,2,0,1:T(8,128)(2,1)}), bf16[2,4,48,1024]{3,2,0,1:T(8,128)(2,1)}, u32[]{:S(2)}, u32[]{:S(2)}) async-start(bf16[2,4,48,1024]{3,2,0,1:T(8,128)(2,1)} %copy.60), calls=%async_computation.1 | async-start | bytes 1572864 | tf_op jit(solution)/shard_map/all_to_all | solution.py:146
  176.4 6.3 %collective-permute-done.21 = bf16[2,1024,128]{2,1,0:T(8,128)(2,1)} collective-permute-done((bf16[2,1024,128]{2,1,0:T(8,128)(2,1)}, bf16[2,1024,128]{2,1,0:T(8,128)(2,1)}, u32[]{:S(2)}, u32[]{:S(2)}) %collective-permute-start.21) | collective-permute-done | bytes 524320 | tf_op jit(solution)/shard_map/ppermute | solution.py:106
  190.8 2.6 %fusion.11 = bf16[256,1024]{1,0:T(8,128)(2,1)} fusion(bf16[384,1024]{1,0:T(8,128)(2,1)} %bitcast.13, bf16[256,1024]{1,0:T(8,128)(2,1)} %copy-done.7, s32[256]{0:T(256)S(1)} %multiply_add_fusion.1), kind=kOutput, calls=%fused_computation.45 | convolution fusion | flops 202211328 | bytes 1836032 | tf_op jit(solution)/shard_map/dot_general | solution.py:26
  193.4 3.0 %bitcast_add_fusion = f32[8,2,32,1536]{3,2,1,0:T(8,128)S(1)} fusion(bf16[8,2,32,1536]{3,2,1,0:T(8,128)(2,1)} %collective-permute-done.10, f32[8,2,2,32,1536]{4,3,2,1,0:T(8,128)} %copy-done.1, s32[]{:T(128)S(6)} %select_n.111), kind=kLoop, calls=%fused_computation | loop fusion | flops 1572864 | bytes 7864324 | tf_op jit(solution)/shard_map/add | solution.py:66
  202.4 19.7 %collective-permute-done.16 = bf16[8,1,32,512]{3,2,1,0:T(8,128)(2,1)S(1)} collective-permute-done((bf16[8,1,32,512]{3,2,1,0:T(8,128)(2,1)S(1)}, bf16[8,1,32,512]{3,2,1,0:T(8,128)(2,1)S(1)}, u32[]{:S(2)}, u32[]{:S(2)}) %collective-permute-start.16) | collective-permute-done | bytes 262176 | tf_op jit(solution)/shard_map/ppermute | solution.py:65
  228.8 7.0 %collective-permute-done.12 = bf16[4,32,1536]{2,1,0:T(8,128)(2,1)S(1)} collective-permute-done((bf16[4,32,1536]{2,1,0:T(8,128)(2,1)S(1)}, bf16[4,32,1536]{2,1,0:T(8,128)(2,1)S(1)}, u32[]{:S(2)}, u32[]{:S(2)}) %collective-permute-start.12) | collective-permute-done | bytes 393248 | tf_op jit(solution)/shard_map/ppermute | solution.py:65
  236.1 4.4 %collective-permute-start.19 = (bf16[1,32,512]{2,1,0:T(8,128)(2,1)S(1)}, bf16[1,32,512]{2,1,0:T(8,128)(2,1)S(1)}, u32[]{:S(2)}, u32[]{:S(2)}) collective-permute-start(bf16[1,32,512]{2,1,0:T(8,128)(2,1)S(1)} %dynamic-slice_convert_fusion.7), channel_id=1, source_target_pairs={{0,16},{4,20},{8,24},{12,28},{16,0},{20,4},{24,8},{28,12},{1,17},{... | collective-permute-start | bytes 98312 | tf_op jit(solution)/shard_map/ppermute | solution.py:65
  242.2 2.7 %collective-permute-start.14 = (bf16[1,32,1536]{2,1,0:T(8,128)(2,1)S(1)}, bf16[1,32,1536]{2,1,0:T(8,128)(2,1)S(1)}, u32[]{:S(2)}, u32[]{:S(2)}) collective-permute-start(bf16[1,32,1536]{2,1,0:T(8,128)(2,1)S(1)} %dynamic-slice_convert_fusion.5), channel_id=1, source_target_pairs={{0,16},{4,20},{8,24},{12,28},{16,0},{20,4},{24,8},{28,12},{1,17},{... | collective-permute-start | bytes 294920 | tf_op jit(solution)/shard_map/ppermute | solution.py:65
  (197 shorter events, 126.9 us)
Async XLA Ops:
  0.6 32.7 %collective-permute-start.1 = (bf16[2,1024,128]{2,1,0:T(8,128)(2,1)}, bf16[2,1024,128]{2,1,0:T(8,128)(2,1)}, u32[]{:S(2)}, u32[]{:S(2)}) collective-permute-start(bf16[2,1024,128]{2,1,0:T(8,128)(2,1)} %param.13), channel_id=1, source_target_pairs={{0,8},{4,12},{8,16},{12,20},{16,24},{20,28},{24,0},{28,4},{1,9},{5... | collective-permute-start | bytes 1572872 | tf_op jit(solution)/shard_map/ppermute | solution.py:98
  3.7 31.3 %collective-permute-start.4 = (bf16[2,128,1024]{2,1,0:T(8,128)(2,1)}, bf16[2,128,1024]{2,1,0:T(8,128)(2,1)}, u32[]{:S(2)}, u32[]{:S(2)}) collective-permute-start(bf16[2,128,1024]{2,1,0:T(8,128)(2,1)} %param.14), channel_id=1, source_target_pairs={{0,8},{4,12},{8,16},{12,20},{16,24},{20,28},{24,0},{28,4},{1,9},{5... | collective-permute-start | bytes 1572872 | tf_op jit(solution)/shard_map/ppermute | solution.py:98
  29.1 15.9 %all-to-all-start = ((bf16[4,2,48,1024]{3,2,1,0:T(8,128)(2,1)}), bf16[4,2,48,1024]{3,2,1,0:T(8,128)(2,1)}, u32[]{:S(2)}, u32[]{:S(2)}) async-start(bf16[4,2,48,1024]{3,2,1,0:T(8,128)(2,1)} %bitcast.159), calls=%async_computation | async-start | bytes 1572864 | tf_op jit(solution)/shard_map/all_to_all | solution.py:138
  33.4 21.4 %collective-permute-start.2 = (bf16[2,1024,128]{2,1,0:T(8,128)(2,1)}, bf16[2,1024,128]{2,1,0:T(8,128)(2,1)}, u32[]{:S(2)}, u32[]{:S(2)}) collective-permute-start(bf16[2,1024,128]{2,1,0:T(8,128)(2,1)} %collective-permute-done.1), channel_id=1, source_target_pairs={{0,8},{4,12},{8,16},{12,20},{16,24},{20,28},{24,0},{28,4},{1,9},{5... | collective-permute-start | bytes 1572872 | tf_op jit(solution)/shard_map/ppermute | solution.py:98
  35.0 26.5 %collective-permute-start.5 = (bf16[2,128,1024]{2,1,0:T(8,128)(2,1)}, bf16[2,128,1024]{2,1,0:T(8,128)(2,1)}, u32[]{:S(2)}, u32[]{:S(2)}) collective-permute-start(bf16[2,128,1024]{2,1,0:T(8,128)(2,1)} %collective-permute-done.4), channel_id=1, source_target_pairs={{0,8},{4,12},{8,16},{12,20},{16,24},{20,28},{24,0},{28,4},{1,9},{5... | collective-permute-start | bytes 1572872 | tf_op jit(solution)/shard_map/ppermute | solution.py:98
  45.1 20.2 %all-to-all-start.2 = ((bf16[4,2,48,1024]{3,2,1,0:T(8,128)(2,1)}), bf16[4,2,48,1024]{3,2,1,0:T(8,128)(2,1)}, u32[]{:S(2)}, u32[]{:S(2)}) async-start(bf16[4,2,48,1024]{3,2,1,0:T(8,128)(2,1)} %bitcast.158), calls=%async_computation.2 | async-start | bytes 1572864 | tf_op jit(solution)/shard_map/all_to_all | solution.py:138
  53.3 32.1 %collective-permute-start = (bf16[2,192,1024]{2,1,0:T(8,128)(2,1)}, bf16[2,192,1024]{2,1,0:T(8,128)(2,1)}, u32[]{:S(2)}, u32[]{:S(2)}) collective-permute-start(bf16[2,192,1024]{2,1,0:T(8,128)(2,1)} %bitcast.9), channel_id=1, source_target_pairs={{0,4},{4,0},{8,12},{12,8},{16,20},{20,16},{24,28},{28,24},{1,5},{5... | collective-permute-start | bytes 2359304 | tf_op jit(solution)/shard_map/ppermute | solution.py:140
  54.8 17.9 %collective-permute-start.3 = (bf16[2,1024,128]{2,1,0:T(8,128)(2,1)}, bf16[2,1024,128]{2,1,0:T(8,128)(2,1)}, u32[]{:S(2)}, u32[]{:S(2)}) collective-permute-start(bf16[2,1024,128]{2,1,0:T(8,128)(2,1)} %collective-permute-done.2), channel_id=1, source_target_pairs={{0,8},{4,12},{8,16},{12,20},{16,24},{20,28},{24,0},{28,4},{1,9},{5... | collective-permute-start | bytes 1572872 | tf_op jit(solution)/shard_map/ppermute | solution.py:98
  61.5 22.0 %collective-permute-start.6 = (bf16[2,128,1024]{2,1,0:T(8,128)(2,1)}, bf16[2,128,1024]{2,1,0:T(8,128)(2,1)}, u32[]{:S(2)}, u32[]{:S(2)}) collective-permute-start(bf16[2,128,1024]{2,1,0:T(8,128)(2,1)} %collective-permute-done.5), channel_id=1, source_target_pairs={{0,8},{4,12},{8,16},{12,20},{16,24},{20,28},{24,0},{28,4},{1,9},{5... | collective-permute-start | bytes 1572872 | tf_op jit(solution)/shard_map/ppermute | solution.py:98
  66.5 23.7 %collective-permute-start.8 = (bf16[2,192,1024]{2,1,0:T(8,128)(2,1)S(1)}, bf16[2,192,1024]{2,1,0:T(8,128)(2,1)S(1)}, u32[]{:S(2)}, u32[]{:S(2)}) collective-permute-start(bf16[2,192,1024]{2,1,0:T(8,128)(2,1)S(1)} %bitcast.174), channel_id=1, source_target_pairs={{0,4},{4,0},{8,12},{12,8},{16,20},{20,16},{24,28},{28,24},{1,5},{5... | collective-permute-start | bytes 2359304 | tf_op jit(solution)/shard_map/ppermute | solution.py:140
  99.6 20.8 %collective-permute-start.9 = (bf16[2,192,1024]{2,1,0:T(8,128)(2,1)}, bf16[2,192,1024]{2,1,0:T(8,128)(2,1)}, u32[]{:S(2)}, u32[]{:S(2)}) collective-permute-start(bf16[2,192,1024]{2,1,0:T(8,128)(2,1)} %slice.45), channel_id=1, source_target_pairs={{0,4},{4,0},{8,12},{12,8},{16,20},{20,16},{24,28},{28,24},{1,5},{5... | collective-permute-start | bytes 2359304 | tf_op jit(solution)/shard_map/ppermute | solution.py:143
  106.3 61.2 %collective-permute-start.7 = (bf16[2,192,1024]{2,1,0:T(8,128)(2,1)}, bf16[2,192,1024]{2,1,0:T(8,128)(2,1)}, u32[]{:S(2)}, u32[]{:S(2)}) collective-permute-start(bf16[2,192,1024]{2,1,0:T(8,128)(2,1)} %slice.46), channel_id=1, source_target_pairs={{0,4},{4,0},{8,12},{12,8},{16,20},{20,16},{24,28},{28,24},{1,5},{5... | collective-permute-start | bytes 2359304 | tf_op jit(solution)/shard_map/ppermute | solution.py:143
  109.3 25.1 %collective-permute-start.23 = (bf16[2,128,1024]{2,1,0:T(8,128)(2,1)}, bf16[2,128,1024]{2,1,0:T(8,128)(2,1)}, u32[]{:S(2)}, u32[]{:S(2)}) collective-permute-start(bf16[2,128,1024]{2,1,0:T(8,128)(2,1)} %split.58), channel_id=1, source_target_pairs={{0,8},{4,12},{8,16},{12,20},{16,24},{20,28},{24,0},{28,4},{1,9},{5... | collective-permute-start | bytes 1572872 | tf_op jit(solution)/shard_map/ppermute | solution.py:106
  122.7 15.9 %all-to-all-start.3 = ((bf16[2,4,48,1024]{3,2,0,1:T(8,128)(2,1)}), bf16[2,4,48,1024]{3,2,0,1:T(8,128)(2,1)}, u32[]{:S(2)}, u32[]{:S(2)}) async-start(bf16[2,4,48,1024]{3,2,0,1:T(8,128)(2,1)} %copy.62), calls=%async_computation.3 | async-start | bytes 1572864 | tf_op jit(solution)/shard_map/all_to_all | solution.py:146
  132.9 30.5 %collective-permute-start.20 = (bf16[2,1024,128]{2,1,0:T(8,128)(2,1)}, bf16[2,1024,128]{2,1,0:T(8,128)(2,1)}, u32[]{:S(2)}, u32[]{:S(2)}) collective-permute-start(bf16[2,1024,128]{2,1,0:T(8,128)(2,1)} %split.59), channel_id=1, source_target_pairs={{0,8},{4,12},{8,16},{12,20},{16,24},{20,28},{24,0},{28,4},{1,9},{5... | collective-permute-start | bytes 1572872 | tf_op jit(solution)/shard_map/ppermute | solution.py:106
  136.8 37.3 %collective-permute-start.24 = (bf16[2,128,1024]{2,1,0:T(8,128)(2,1)}, bf16[2,128,1024]{2,1,0:T(8,128)(2,1)}, u32[]{:S(2)}, u32[]{:S(2)}) collective-permute-start(bf16[2,128,1024]{2,1,0:T(8,128)(2,1)} %fusion.34), channel_id=1, source_target_pairs={{0,8},{4,12},{8,16},{12,20},{16,24},{20,28},{24,0},{28,4},{1,9},{5... | collective-permute-start | bytes 1572872 | tf_op jit(solution)/shard_map/ppermute | solution.py:106
  163.4 30.0 %collective-permute-start.10 = (bf16[8,2,32,1536]{3,2,1,0:T(8,128)(2,1)}, bf16[8,2,32,1536]{3,2,1,0:T(8,128)(2,1)}, u32[]{:S(2)}, u32[]{:S(2)}) collective-permute-start(bf16[8,2,32,1536]{3,2,1,0:T(8,128)(2,1)} %fusion.7), channel_id=1, source_target_pairs={{0,1},{1,0},{2,3},{3,2},{4,5},{5,4},{6,7},{7,6},{8,9},{9,8},{10,11... | collective-permute-start | bytes 4718600 | tf_op jit(solution)/shard_map/ppermute | solution.py:65
  165.9 16.9 %collective-permute-start.21 = (bf16[2,1024,128]{2,1,0:T(8,128)(2,1)}, bf16[2,1024,128]{2,1,0:T(8,128)(2,1)}, u32[]{:S(2)}, u32[]{:S(2)}) collective-permute-start(bf16[2,1024,128]{2,1,0:T(8,128)(2,1)} %fusion.36), channel_id=1, source_target_pairs={{0,8},{4,12},{8,16},{12,20},{16,24},{20,28},{24,0},{28,4},{1,9},{5... | collective-permute-start | bytes 1572872 | tf_op jit(solution)/shard_map/ppermute | solution.py:106
  169.8 21.0 %all-to-all-start.1 = ((bf16[2,4,48,1024]{3,2,0,1:T(8,128)(2,1)}), bf16[2,4,48,1024]{3,2,0,1:T(8,128)(2,1)}, u32[]{:S(2)}, u32[]{:S(2)}) async-start(bf16[2,4,48,1024]{3,2,0,1:T(8,128)(2,1)} %copy.60), calls=%async_computation.1 | async-start | bytes 1572864 | tf_op jit(solution)/shard_map/all_to_all | solution.py:146
  176.3 23.6 %collective-permute-start.25 = (bf16[2,128,1024]{2,1,0:T(8,128)(2,1)}, bf16[2,128,1024]{2,1,0:T(8,128)(2,1)}, u32[]{:S(2)}, u32[]{:S(2)}) collective-permute-start(bf16[2,128,1024]{2,1,0:T(8,128)(2,1)} %fusion.33), channel_id=1, source_target_pairs={{0,8},{4,12},{8,16},{12,20},{16,24},{20,28},{24,0},{28,4},{1,9},{5... | collective-permute-start | bytes 1572872 | tf_op jit(solution)/shard_map/ppermute | solution.py:106
  185.0 39.6 %collective-permute-start.22 = (bf16[2,1024,128]{2,1,0:T(8,128)(2,1)}, bf16[2,1024,128]{2,1,0:T(8,128)(2,1)}, u32[]{:S(2)}, u32[]{:S(2)}) collective-permute-start(bf16[2,1024,128]{2,1,0:T(8,128)(2,1)} %fusion.35), channel_id=1, source_target_pairs={{0,8},{4,12},{8,16},{12,20},{16,24},{20,28},{24,0},{28,4},{1,9},{5... | collective-permute-start | bytes 1572872 | tf_op jit(solution)/shard_map/ppermute | solution.py:106
  196.5 27.3 %collective-permute-start.11 = (bf16[8,1,32,1536]{3,2,1,0:T(8,128)(2,1)S(1)}, bf16[8,1,32,1536]{3,2,1,0:T(8,128)(2,1)S(1)}, u32[]{:S(2)}, u32[]{:S(2)}) collective-permute-start(bf16[8,1,32,1536]{3,2,1,0:T(8,128)(2,1)S(1)} %dynamic-slice_convert_fusion.1), channel_id=1, source_target_pairs={{0,2},{1,3},{2,0},{3,1},{4,6},{5,7},{6,4},{7,5},{8,10},{9,11},{10,... | collective-permute-start | bytes 2359304 | tf_op jit(solution)/shard_map/ppermute | solution.py:65
  198.0 24.1 %collective-permute-start.16 = (bf16[8,1,32,512]{3,2,1,0:T(8,128)(2,1)S(1)}, bf16[8,1,32,512]{3,2,1,0:T(8,128)(2,1)S(1)}, u32[]{:S(2)}, u32[]{:S(2)}) collective-permute-start(bf16[8,1,32,512]{3,2,1,0:T(8,128)(2,1)S(1)} %dynamic-slice_convert_fusion.3), channel_id=1, source_target_pairs={{0,2},{1,3},{2,0},{3,1},{4,6},{5,7},{6,4},{7,5},{8,10},{9,11},{10,... | collective-permute-start | bytes 786440 | tf_op jit(solution)/shard_map/ppermute | solution.py:65
  224.1 11.8 %collective-permute-start.12 = (bf16[4,32,1536]{2,1,0:T(8,128)(2,1)S(1)}, bf16[4,32,1536]{2,1,0:T(8,128)(2,1)S(1)}, u32[]{:S(2)}, u32[]{:S(2)}) collective-permute-start(bf16[4,32,1536]{2,1,0:T(8,128)(2,1)S(1)} %fusion.48), channel_id=1, source_target_pairs={{0,4},{4,0},{8,12},{12,8},{16,20},{20,16},{24,28},{28,24},{1,5},{5... | collective-permute-start | bytes 1179656 | tf_op jit(solution)/shard_map/ppermute | solution.py:65
  (41 other events, 190.6 us)

commit v2 on v1

v2 whole, which is shorter than its diff:
```python
import jax
import jax.numpy as jnp
from jax import lax
from jax.experimental import pallas as pl
from jax.experimental.pallas import tpu as pltpu
from jax.sharding import PartitionSpec as P

HD = 64


EPSILON = 1e-06


def rms_norm(values):
    scale = lax.rsqrt(jnp.mean(values * values, axis=-1, keepdims=True) + EPSILON)
    return (values * scale).astype(jnp.bfloat16)


def gelu_tanh(values):
    return jax.nn.gelu(values, approximate=True)


def gelu_back(pre_act, cotangent):
    return jax.vjp(gelu_tanh, pre_act)[1](cotangent)[0]


def row_contract(left, right):
    return lax.dot_general(
        left, right, (((0,), (0,)), ((), ())), preferred_element_type=jnp.float32
    )


def col_contract(left, right):
    return lax.dot_general(
        left, right, (((1,), (1,)), ((), ())), preferred_element_type=jnp.float32
    )


def softmax_parts(packed_ref, rows, pair, side, width, same, first):
    query = packed_ref[rows, pl.ds(pair * 128, 128)]
    keys = packed_ref[rows, pl.ds(width + pair * 128, 128)]
    mine = first if side == 0 else jnp.logical_not(first)
    query = jnp.where(mine, query, jnp.zeros_like(query))
    scores = col_contract(query, keys) * HD ** (-0.5)
    weights = jnp.where(same, jnp.exp(scores), 0.0)
    return weights / jnp.sum(weights, axis=-1, keepdims=True)


def first_half():
    return lax.broadcasted_iota(jnp.int32, (128, 128), 1) < HD


def front_kernel(x_ref, col_ref, row_ref, qkv_ref, wo_ref, normed_ref, packed_ref, mixed_ref, resid_ref, inner_ref):
    width = mixed_ref.shape[1]
    first = first_half()
    normed_ref[...] = rms_norm(x_ref[...].astype(jnp.float32))
    packed_ref[...] = jnp.dot(
        normed_ref[...], qkv_ref[...], preferred_element_type=jnp.float32
    ).astype(jnp.bfloat16)
    for block in range(x_ref.shape[0] // 128):
        rows = pl.ds(block * 128, 128)
        same = col_ref[rows, :] == row_ref[:, rows]
        for pair in range(width // 128):
            values = packed_ref[rows, pl.ds(2 * width + pair * 128, 128)]
            heads = []
            for side in range(2):
                probs = softmax_parts(packed_ref, rows, pair, side, width, same, first)
                heads.append(
                    jnp.dot(probs.astype(jnp.bfloat16), values, preferred_element_type=jnp.float32)
                )
            mixed_ref[rows, pl.ds(pair * 128, 128)] = jnp.where(first, heads[0], heads[1]).astype(
                jnp.bfloat16
            )
    resid = (x_ref[...].astype(jnp.float32) + col_contract(mixed_ref[...], wo_ref[...])).astype(
        jnp.bfloat16
    )
    resid_ref[...] = resid
    inner_ref[...] = rms_norm(resid.astype(jnp.float32))


def back_kernel(grad_ref, col_ref, row_ref, wo_ref, packed_ref, out_ref, mixed_grad_ref):
    width = wo_ref.shape[1]
    first = first_half()
    mixed_grad_ref[...] = jnp.dot(
        grad_ref[...], wo_ref[...], preferred_element_type=jnp.float32
    ).astype(jnp.bfloat16)
    for block in range(grad_ref.shape[0] // 128):
        rows = pl.ds(block * 128, 128)
        same = col_ref[rows, :] == row_ref[:, rows]
        for pair in range(width // 128):
            query = packed_ref[rows, pl.ds(pair * 128, 128)]
            keys = packed_ref[rows, pl.ds(width + pair * 128, 128)]
            values = packed_ref[rows, pl.ds(2 * width + pair * 128, 128)]
            d_mixed = mixed_grad_ref[rows, pl.ds(pair * 128, 128)]
            parts = []
            for side in range(2):
                mine = first if side == 0 else jnp.logical_not(first)
                probs = softmax_parts(packed_ref, rows, pair, side, width, same, first)
                d_values = row_contract(probs.astype(jnp.bfloat16), d_mixed)
                d_probs = col_contract(jnp.where(mine, d_mixed, jnp.zeros_like(d_mixed)), values)
                d_probs = d_probs.astype(jnp.bfloat16).astype(jnp.float32)
                inside = jnp.sum(d_probs * probs, axis=-1, keepdims=True)
                d_scores = (probs * (d_probs - inside) * HD ** (-0.5)).astype(jnp.bfloat16)
                d_query = jnp.dot(d_scores, keys, preferred_element_type=jnp.float32)
                d_keys = row_contract(d_scores, query)
                parts.append((d_query, d_keys, d_values))
            for at, (left, right) in enumerate(zip(*parts)):
                out_ref[rows, pl.ds(at * width + pair * 128, 128)] = jnp.where(
                    first, left, right
                ).astype(jnp.bfloat16)


def front(x, col, row, w_qkv, w_o):
    rows, width = x.shape[0], w_o.shape[1]
    shape = lambda cols: jax.ShapeDtypeStruct((rows, cols), jnp.bfloat16)
    return pl.pallas_call(
        front_kernel,
        out_shape=[shape(x.shape[1]), shape(3 * width), shape(width), shape(x.shape[1]), shape(x.shape[1])],
        compiler_params=pltpu.CompilerParams(vmem_limit_bytes=40 * 1024 * 1024),
        cost_estimate=pl.CostEstimate(flops=6 * 10**9, bytes_accessed=7 * 10**6, transcendentals=0),
        name="front",
    )(x, col, row, w_qkv, w_o)


def attention_back(d_resid, col, row, w_o, packed):
    return pl.pallas_call(
        back_kernel,
        out_shape=jax.ShapeDtypeStruct(packed.shape, jnp.bfloat16),
        scratch_shapes=[pltpu.VMEM((packed.shape[0], w_o.shape[1]), jnp.bfloat16)],
        compiler_params=pltpu.CompilerParams(vmem_limit_bytes=40 * 1024 * 1024),
        cost_estimate=pl.CostEstimate(flops=6 * 10**9, bytes_accessed=7 * 10**6, transcendentals=0),
        name="attention_back",
    )(d_resid, col, row, w_o, packed)


def norm_back(values, cotangent):
    scale = lax.rsqrt(jnp.mean(values * values, axis=-1, keepdims=True) + EPSILON)
    along = jnp.mean(values * cotangent, axis=-1, keepdims=True)
    return scale * (cotangent - values * (scale * scale * along))


def stage_perm(count, bit):
    return [(i, i ^ bit) for i in range(count)]


def halve(values, axis_name, count, axis, bit):
    own = (lax.axis_index(axis_name) // bit) % 2
    keep = lax.dynamic_index_in_dim(values, own, axis, keepdims=True)
    give = lax.dynamic_index_in_dim(values, 1 - own, axis, keepdims=True).astype(jnp.bfloat16)
    came = lax.ppermute(give, axis_name, stage_perm(count, bit))
    return keep + came.astype(jnp.float32)


def scatter_sum(term, late_y):
    groups, shards = lax.axis_size("dp"), lax.axis_size("expert")
    rows, cols = term.shape
    bits = []
    for name, count in (("dp", groups), ("expert", shards)):
        bit = count // 2
        while bit:
            bits.append((name, count, bit))
            bit //= 2
    value = term.reshape((2,) * len(bits) + (rows // (groups * shards), cols))
    expert_bits = [b for b in reversed(bits) if b[0] == "expert"]
    group_bits = [b for b in reversed(bits) if b[0] == "dp"]
    if late_y:
        order = expert_bits[:1] + group_bits[:1] + expert_bits[1:] + group_bits[1:]
    else:
        order = expert_bits + group_bits
    for one in order:
        value = halve(value, one[0], one[1], bits.index(one), one[2])
    return value.reshape(rows // (groups * shards), cols)


def ring_pairs(groups, step):
    half = groups // 2
    return [(i, ((i // 2 + step) % half) * 2 + i % 2) for i in range(groups)]


def gather_step(slots, pairs):
    return slots + [lax.ppermute(slots[-1], "dp", pairs)]


def reduce_step(total, slots, step, pairs):
    came = lax.ppermute(total.astype(jnp.bfloat16), "dp", pairs)
    return came.astype(jnp.float32) + slots[(step + 2) % len(slots)]


def on_device(layer_in, body_of, expert_of, w_qkv, w_o, w_up, w_down, d_out):
    tok_rows = layer_in.shape[0]
    width = layer_in.shape[1]
    shards = lax.axis_size("expert")
    groups = lax.axis_size("dp")
    half = groups // 2
    local_experts = w_up.shape[0]
    all_experts = local_experts * shards
    capacity = 3 * tok_rows // (2 * all_experts)
    received = shards * capacity
    partner = stage_perm(groups, 1)
    forth, back = ring_pairs(groups, 1), ring_pairs(groups, -1)

    ups, downs = gather_step([w_up], forth), gather_step([w_down], forth)

    ids = expert_of[:, 0]
    at = jnp.arange(tok_rows, dtype=jnp.int32)
    earlier = (ids[:, None] == ids[None, :]) & (at[None, :] < at[:, None])
    ranks = jnp.sum(earlier.astype(jnp.int32), axis=1)
    slots = ids * capacity + ranks
    places = jnp.arange(all_experts * capacity, dtype=jnp.int32)
    spread = (places[:, None] == slots[None, :]).astype(jnp.bfloat16)

    def to_slots(values):
        store = jnp.dot(spread, values, preferred_element_type=jnp.float32).astype(jnp.bfloat16)
        return store.reshape(shards, local_experts, capacity, width)

    def exchange(store):
        sent = lax.all_to_all(store, "expert", split_axis=0, concat_axis=2, tiled=True)
        return sent.reshape(local_experts, received, width)

    def with_partner(own):
        return jnp.concatenate([own, lax.ppermute(own, "dp", partner)], axis=1)

    def to_tokens(values):
        other = lax.ppermute(values[:, received:].astype(jnp.bfloat16), "dp", partner)
        total = (values[:, :received] + other.astype(jnp.float32)).astype(jnp.bfloat16)
        total = total.reshape(local_experts, shards, capacity, width)
        returned = lax.all_to_all(total, "expert", split_axis=1, concat_axis=0, tiled=True)
        returned = returned.reshape(all_experts * capacity, width)
        return row_contract(spread, returned)

    col, row = body_of[:, None], body_of[None, :]
    store, layer_in = lax.optimization_barrier((to_slots(d_out), layer_in))
    own_grads = exchange(store)
    normed, packed, mixed, resid, inner = front(layer_in, col, row, w_qkv, w_o)
    store, own_grads, ups, downs = lax.optimization_barrier((to_slots(inner), own_grads, ups, downs))
    ups, downs = gather_step(ups, forth), gather_step(downs, forth)
    grads_in = with_partner(own_grads)
    own_inputs, ups, downs = lax.optimization_barrier((exchange(store), ups, downs))
    inputs = with_partner(own_inputs)
    while len(ups) < half:
        ups, downs = gather_step(ups, forth), gather_step(downs, forth)
    full_up = jnp.concatenate(ups, axis=2)
    full_down = jnp.concatenate(downs, axis=1)
    d_hidden = jnp.einsum("esd,efd->esf", grads_in, full_down, preferred_element_type=jnp.float32)
    pre_act = jnp.einsum("esd,edf->esf", inputs, full_up, preferred_element_type=jnp.float32)
    hidden = gelu_tanh(pre_act).astype(jnp.bfloat16)
    d_pre = gelu_back(pre_act, d_hidden).astype(jnp.bfloat16)
    d_inputs = jnp.einsum("esf,edf->esd", d_pre, full_up, preferred_element_type=jnp.float32)
    d_inner = to_tokens(d_inputs).astype(jnp.bfloat16)
    part_down = jnp.einsum("esf,esd->efd", hidden, grads_in, preferred_element_type=jnp.float32)
    part_up = jnp.einsum("esd,esf->edf", inputs, d_pre, preferred_element_type=jnp.float32)
    slots_up = jnp.split(part_up, half, axis=2)
    slots_down = jnp.split(part_down, half, axis=1)
    grad_up = reduce_step(slots_up[1], slots_up, 0, forth)
    grad_down = reduce_step(slots_down[1], slots_down, 0, forth)
    result = jnp.einsum("esf,efd->esd", hidden, full_down, preferred_element_type=jnp.float32)
    expert_out = to_tokens(result)
    out = (resid.astype(jnp.float32) + expert_out).astype(jnp.bfloat16)
    d_inner, grad_up, grad_down = lax.optimization_barrier((d_inner, grad_up, grad_down))
    grad_up = reduce_step(grad_up, slots_up, 1, forth)
    grad_down = reduce_step(grad_down, slots_down, 1, forth)
    resid_grad = norm_back(resid.astype(jnp.float32), d_inner.astype(jnp.float32))
    d_resid = (d_out.astype(jnp.float32) + resid_grad).astype(jnp.bfloat16)
    grad_o = scatter_sum(row_contract(d_resid, mixed), True)
    d_packed = attention_back(d_resid, col, row, w_o, packed)
    d_packed, grad_up, grad_down = lax.optimization_barrier((d_packed, grad_up, grad_down))
    for step in range(2, half - 1):
        grad_up = reduce_step(grad_up, slots_up, step, forth)
        grad_down = reduce_step(grad_down, slots_down, step, forth)
    split = d_packed.shape[1] // 2
    grad_qkv = jnp.concatenate(
        [
            scatter_sum(row_contract(normed, d_packed[:, :split]), False),
            scatter_sum(row_contract(normed, d_packed[:, split:]), True),
        ],
        axis=1,
    )
    d_normed = col_contract(d_packed, w_qkv).astype(jnp.bfloat16)
    input_grad = norm_back(layer_in.astype(jnp.float32), d_normed.astype(jnp.float32))
    grad_input = (d_resid.astype(jnp.float32) + input_grad).astype(jnp.bfloat16)
    return (out, grad_input, grad_qkv, grad_o, grad_up, grad_down)


def solution(mesh):
    in_specs = (
        P(("dp", "expert"), None),
        P(("dp", "expert")),
        P(("dp", "expert"), None),
        P(),
        P(),
        P("expert", None, "dp"),
        P("expert", "dp", None),
        P(("dp", "expert"), None),
    )
    out_specs = (
        P(("dp", "expert"), None),
        P(("dp", "expert"), None),
        P(("dp", "expert"), None),
        P(("dp", "expert"), None),
        P("expert", None, "dp"),
        P("expert", "dp", None),
    )
    return jax.shard_map(
        on_device, mesh=mesh, in_specs=in_specs, out_specs=out_specs, check_vma=False
    )
```

time: 251 us -> 245 us (0.976)
  waiting for transfers between devices: 73.1 us -> 131 us
  local copies, waits for them, and re-layouts: 57.9 us -> 24.3 us
  matrix products: 40.9 us -> 16.9 us
  Pallas kernels: 0 us -> 11.2 us
  starting transfers between devices: 46.4 us -> 37.8 us
  other arithmetic: 28.9 us -> 20.9 us
    ppermute x14, waiting for transfers between devices: 22.2 us -> 50.2 us  [the longest x6 37.7 us: gather_step(): return slots + [lax.ppermute(slots[-1], 'dp', pairs)]]
    ppermute x2, waiting for transfers between devices: 9.45 us -> 24.1 us  [to_tokens(): lax.ppermute(values[:, received:].astype(jnp.bfloat16), 'dp', partner)]
    unnamed x79 -> x42, local copies, waits for them, and re-layouts: 28.1 us -> 15.2 us
    pallas_call x0 -> x2, Pallas kernels: none -> 11.2 us  [the longest x1 5.85 us: attention_back(): pl.pallas_call(back_kernel, out_shape=jax.ShapeDtypeStruct(packed.shape,...]
    ppermute x10 -> x15, waiting for transfers between devices: 32.1 us -> 42.4 us  [halve(): came = lax.ppermute(give, axis_name, stage_perm(count, bit))]
    dot_general x10 -> x2, matrix products: 13.7 us -> 3.55 us  [to_slots(): jnp.dot(spread, values, preferred_element_type=jnp.float32)]
    convert_element_type x6 -> x2, other arithmetic: 9.85 us -> 1.47 us  [the longest x1 1.14 us: on_device(): grad_input = (d_resid.astype(jnp.float32) + input_grad).astype(jnp.bfloat16)]
    add x2 -> x6, other arithmetic: 4.95 us -> 12.6 us  [reduce_step(): return came.astype(jnp.float32) + slots[(step + 2) % len(slots)]]
  transfers between devices with their start and end apart: 30 -> 35, of which waited for: 13 -> 24; matrix products, arithmetic and copies ran while one was open for 43% -> 19% of each run, Pallas kernels for 0% -> 5%
where the time goes in v2:
time: 245 us; the launch traced here: 244 us
  waiting for transfers between devices  131 us (53%)
  starting transfers between devices  37.8 us (15%)
  local copies, waits for them, and re-layouts  24.3 us (10%)
  other arithmetic  20.9 us (9%)
  matrix products  16.9 us (7%)
  Pallas kernels  11.2 us (5%)
    ppermute x15, waiting for transfers between devices, halve(): came = lax.ppermute(give, axis_name, stage_perm(count, bit))  42.4 us
    ppermute x6, waiting for transfers between devices, gather_step(): return slots + [lax.ppermute(slots[-1], 'dp', pairs)]  37.7 us
    ppermute x2, waiting for transfers between devices, to_tokens(): lax.ppermute(values[:, received:].astype(jnp.bfloat16), 'dp', partner)  24.1 us
    unnamed x42, local copies, waits for them, and re-layouts  15.2 us
    add x6, other arithmetic, reduce_step(): return came.astype(jnp.float32) + slots[(step + 2) % len(slots)]  12.6 us
    ppermute x6, waiting for transfers between devices, reduce_step(): came = lax.ppermute(total.astype(jnp.bfloat16), 'dp', pairs)  12.4 us
    ppermute x15, starting transfers between devices, halve(): came = lax.ppermute(give, axis_name, stage_perm(count, bit))  10.6 us
    all_to_all x2, waiting for transfers between devices, exchange(): lax.all_to_all(store, 'expert', split_axis=0, concat_axis=2, tiled=True)  9.4 us
  transfers between devices with their start and end apart: 35, of which 24 were waited for; matrix products, arithmetic and copies ran while one was open for 19% of the time, Pallas kernels for 5%

profile of v2, /device:TPU:0, one launch (start us, length us, event | category | flops | bytes accessed | tf_op | source)
XLA Modules:
  0.0 243.7 jit_solution(1723980005119159829)
XLA Ops:
  0.7 3.1 %collective-permute-start = (bf16[2,1024,128]{2,1,0:T(8,128)(2,1)}, bf16[2,1024,128]{2,1,0:T(8,128)(2,1)}, u32[]{:S(2)}, u32[]{:S(2)}) collective-permute-start(bf16[2,1024,128]{2,1,0:T(8,128)(2,1)} %param.13), channel_id=1, source_target_pairs={{0,8},{4,12},{8,16},{12,20},{16,24},{20,28},{24,0},{28,4},{1,9},{5... | collective-permute-start | bytes 1572872 | tf_op jit(solution)/shard_map/ppermute | solution.py:181
  9.2 3.5 %all-to-all-start = ((bf16[4,2,48,1024]{3,2,1,0:T(8,128)(2,1)}), bf16[4,2,48,1024]{3,2,1,0:T(8,128)(2,1)S(1)}, u32[]{:S(2)}, u32[]{:S(2)}) async-start(bf16[4,2,48,1024]{3,2,1,0:T(8,128)(2,1)} %bitcast.1), calls=%async_computation | async-start | bytes 1572864 | tf_op jit(solution)/shard_map/all_to_all | solution.py:217
  16.0 5.3 %front.1 = (bf16[256,1024]{1,0:T(8,128)(2,1)S(1)}, bf16[256,1536]{1,0:T(8,128)(2,1)S(1)}, bf16[256,512]{1,0:T(8,128)(2,1)S(1)}, bf16[256,1024]{1,0:T(8,128)(2,1)S(1)}, bf16[256,1024]{1,0:T(8,128)(2,1)S(1)}) custom-call(bf16[256,1024]{1,0:T(8,128)(2,1)S(1)} %copy-done, s32[256,1]{1,0:T(8,128)S(1)} %copy.26.col_ref, s32[1,256]{1,0:T(1,128)S(1)} %bitcast.55, ...), custom_call_target="tpu_custom_call" | custom-call | flops 6000000000 | bytes 7000000 | tf_op jit(solution)/shard_map/front/pallas_call | solution.py:116
  25.3 3.9 %collective-permute-done.1 = bf16[2,128,1024]{2,1,0:T(8,128)(2,1)} collective-permute-done((bf16[2,128,1024]{2,1,0:T(8,128)(2,1)}, bf16[2,128,1024]{2,1,0:T(8,128)(2,1)}, u32[]{:S(2)}, u32[]{:S(2)}) %collective-permute-start.1) | collective-permute-done | bytes 524320 | tf_op jit(solution)/shard_map/ppermute | solution.py:181
  29.2 4.2 %all-to-all-start.1 = ((bf16[4,2,48,1024]{3,2,1,0:T(8,128)(2,1)}), bf16[4,2,48,1024]{3,2,1,0:T(8,128)(2,1)}, u32[]{:S(2)}, u32[]{:S(2)}) async-start(bf16[4,2,48,1024]{3,2,1,0:T(8,128)(2,1)} %bitcast.4), calls=%async_computation.1 | async-start | bytes 1572864 | tf_op jit(solution)/shard_map/all_to_all | solution.py:217
  37.5 7.7 %all-to-all-done.1 = bf16[4,2,48,1024]{3,2,1,0:T(8,128)(2,1)} async-done(((bf16[4,2,48,1024]{3,2,1,0:T(8,128)(2,1)}), bf16[4,2,48,1024]{3,2,1,0:T(8,128)(2,1)}, u32[]{:S(2)}, u32[]{:S(2)}) %all-to-all-start.1) | async-done | bytes 786464 | tf_op jit(solution)/shard_map/all_to_all | solution.py:217
  46.4 3.9 %collective-permute-done.2 = bf16[2,1024,128]{2,1,0:T(8,128)(2,1)} collective-permute-done((bf16[2,1024,128]{2,1,0:T(8,128)(2,1)}, bf16[2,1024,128]{2,1,0:T(8,128)(2,1)}, u32[]{:S(2)}, u32[]{:S(2)}) %collective-permute-start.2) | collective-permute-done | bytes 524320 | tf_op jit(solution)/shard_map/ppermute | solution.py:181
  50.3 10.8 %collective-permute-done.3 = bf16[2,128,1024]{2,1,0:T(8,128)(2,1)} collective-permute-done((bf16[2,128,1024]{2,1,0:T(8,128)(2,1)}, bf16[2,128,1024]{2,1,0:T(8,128)(2,1)}, u32[]{:S(2)}, u32[]{:S(2)}) %collective-permute-start.3) | collective-permute-done | bytes 524320 | tf_op jit(solution)/shard_map/ppermute | solution.py:181
  68.6 9.4 %collective-permute-done.5 = bf16[2,1024,128]{2,1,0:T(8,128)(2,1)S(1)} collective-permute-done((bf16[2,1024,128]{2,1,0:T(8,128)(2,1)}, bf16[2,1024,128]{2,1,0:T(8,128)(2,1)S(1)}, u32[]{:S(2)}, u32[]{:S(2)}) %collective-permute-start.5) | collective-permute-done | bytes 524320 | tf_op jit(solution)/shard_map/ppermute | solution.py:181
  78.1 9.7 %collective-permute-done.6 = bf16[2,128,1024]{2,1,0:T(8,128)(2,1)S(1)} collective-permute-done((bf16[2,128,1024]{2,1,0:T(8,128)(2,1)}, bf16[2,128,1024]{2,1,0:T(8,128)(2,1)S(1)}, u32[]{:S(2)}, u32[]{:S(2)}) %collective-permute-start.6) | collective-permute-done | bytes 524320 | tf_op jit(solution)/shard_map/ppermute | solution.py:181
  104.0 24.1 %collective-permute-done.9 = bf16[2,192,1024]{2,1,0:T(8,128)(2,1)S(1)} collective-permute-done((bf16[2,192,1024]{2,1,0:T(8,128)(2,1)S(1)}, bf16[2,192,1024]{2,1,0:T(8,128)(2,1)S(1)}, u32[]{:S(2)}, u32[]{:S(2)}) %collective-permute-start.9) | collective-permute-done | bytes 786464 | tf_op jit(solution)/shard_map/ppermute | solution.py:224
  129.3 3.5 %all-to-all-start.3 = ((bf16[2,4,48,1024]{3,2,0,1:T(8,128)(2,1)}), bf16[2,4,48,1024]{3,2,0,1:T(8,128)(2,1)S(1)}, u32[]{:S(2)}, u32[]{:S(2)}) async-start(bf16[2,4,48,1024]{3,2,0,1:T(8,128)(2,1)} %copy.30), calls=%async_computation.3 | async-start | bytes 1572864 | tf_op jit(solution)/shard_map/all_to_all | solution.py:227
  132.8 2.5 %slice_add_fusion.6 = bf16[2,128,1024]{2,1,0:T(8,128)(2,1)} fusion(f32[2,512,1024]{2,1,0:T(8,128)} %copy-done.8, bf16[2,128,1024]{2,1,0:T(8,128)(2,1)} %collective-permute-done.11), kind=kLoop, calls=%fused_computation.48 | loop fusion | flops 786432 | bytes 2097152 | tf_op jit(solution)/shard_map/add | solution.py:186
  139.9 4.5 %all-to-all-done.3 = bf16[2,4,48,1024]{3,2,0,1:T(8,128)(2,1)S(1)} async-done(((bf16[2,4,48,1024]{3,2,0,1:T(8,128)(2,1)}), bf16[2,4,48,1024]{3,2,0,1:T(8,128)(2,1)S(1)}, u32[]{:S(2)}, u32[]{:S(2)}) %all-to-all-start.3) | async-done | bytes 786464 | tf_op jit(solution)/shard_map/all_to_all | solution.py:227
  144.4 4.2 %all-to-all-start.2 = ((bf16[2,4,48,1024]{3,2,0,1:T(8,128)(2,1)}), bf16[2,4,48,1024]{3,2,0,1:T(8,128)(2,1)}, u32[]{:S(2)}, u32[]{:S(2)}) async-start(bf16[2,4,48,1024]{3,2,0,1:T(8,128)(2,1)} %copy.29), calls=%async_computation.2 | async-start | bytes 1572864 | tf_op jit(solution)/shard_map/all_to_all | solution.py:227
  150.8 5.9 %attention_back.1 = bf16[256,1536]{1,0:T(8,128)(2,1)S(1)} custom-call(bf16[256,1024]{1,0:T(8,128)(2,1)S(1)} %fusion.12.grad_ref, s32[256,1]{1,0:T(8,128)S(1)} %copy.26.col_ref, s32[1,256]{1,0:T(1,128)S(1)} %bitcast.56, bf16[1024,512]{1,0:T(8,128)(2,1)S(1)} %copy-done.5, bf16[256,1536]{1,0:T(8,128)(2,1)S(1)} %copy-done.7), custom_call_target="tpu_custom_call" | custom-call | flops 6000000000 | bytes 7000000 | tf_op jit(solution)/shard_map/attention_back/pallas_call | solution.py:126
  162.8 3.3 %collective-permute-done.12 = bf16[2,1024,128]{2,1,0:T(8,128)(2,1)} collective-permute-done((bf16[2,1024,128]{2,1,0:T(8,128)(2,1)}, bf16[2,1024,128]{2,1,0:T(8,128)(2,1)}, u32[]{:S(2)}, u32[]{:S(2)}) %collective-permute-start.12) | collective-permute-done | bytes 524320 | tf_op jit(solution)/shard_map/ppermute | solution.py:185
  167.7 9.2 %collective-permute-done.13 = bf16[2,128,1024]{2,1,0:T(8,128)(2,1)} collective-permute-done((bf16[2,128,1024]{2,1,0:T(8,128)(2,1)}, bf16[2,128,1024]{2,1,0:T(8,128)(2,1)}, u32[]{:S(2)}, u32[]{:S(2)}) %collective-permute-start.13) | collective-permute-done | bytes 524320 | tf_op jit(solution)/shard_map/ppermute | solution.py:185
  184.2 4.9 %collective-permute-done.25 = bf16[2,2,1,2,1,32,512]{6,5,4,3,2,1,0:T(8,128)(2,1)S(1)} collective-permute-done((bf16[2,2,1,2,1,32,512]{6,5,4,3,2,1,0:T(8,128)(2,1)S(1)}, bf16[2,2,1,2,1,32,512]{6,5,4,3,2,1,0:T(8,128)(2,1)S(1)}, u32[]{:S(2)}, u32[]{:S(2)}) %collective-permute-start.25) | collective-permute-done | bytes 262176 | tf_op jit(solution)/shard_map/ppermute | solution.py:150
  190.8 3.5 %collective-permute-done.26 = bf16[2,2,1,1,1,32,512]{6,5,4,3,2,1,0:T(8,128)(2,1)S(1)} collective-permute-done((bf16[2,2,1,1,1,32,512]{6,5,4,3,2,1,0:T(8,128)(2,1)S(1)}, bf16[2,2,1,1,1,32,512]{6,5,4,3,2,1,0:T(8,128)(2,1)S(1)}, u32[]{:S(2)}, u32[]{:S(2)}) %collective-permute-start.26) | collective-permute-done | bytes 131104 | tf_op jit(solution)/shard_map/ppermute | solution.py:150
  194.4 11.9 %collective-permute-done.27 = bf16[2,1,1,1,1,32,512]{6,5,4,3,2,1,0:T(8,128)(2,1)S(1)} collective-permute-done((bf16[2,1,1,1,1,32,512]{6,5,4,3,2,1,0:T(8,128)(2,1)S(1)}, bf16[2,1,1,1,1,32,512]{6,5,4,3,2,1,0:T(8,128)(2,1)S(1)}, u32[]{:S(2)}, u32[]{:S(2)}) %collective-permute-start.27) | collective-permute-done | bytes 65568 | tf_op jit(solution)/shard_map/ppermute | solution.py:150
  208.1 3.1 %collective-permute-done.28 = bf16[1,1,1,1,1,32,512]{6,5,4,3,2,1,0:T(8,128)(2,1)S(1)} collective-permute-done((bf16[1,1,1,1,1,32,512]{6,5,4,3,2,1,0:T(8,128)(2,1)S(1)}, bf16[1,1,1,1,1,32,512]{6,5,4,3,2,1,0:T(8,128)(2,1)S(1)}, u32[]{:S(2)}, u32[]{:S(2)}) %collective-permute-start.28) | collective-permute-done | bytes 32800 | tf_op jit(solution)/shard_map/ppermute | solution.py:150
  220.0 4.7 %collective-permute-done.20 = bf16[2,2,1,2,1,32,768]{6,5,4,3,2,1,0:T(8,128)(2,1)S(1)} collective-permute-done((bf16[2,2,1,2,1,32,768]{6,5,4,3,2,1,0:T(8,128)(2,1)S(1)}, bf16[2,2,1,2,1,32,768]{6,5,4,3,2,1,0:T(8,128)(2,1)S(1)}, u32[]{:S(2)}, u32[]{:S(2)}) %collective-permute-start.20) | collective-permute-done | bytes 393248 | tf_op jit(solution)/shard_map/ppermute | solution.py:150
  227.9 2.6 %collective-permute-done.21 = bf16[2,2,1,1,1,32,768]{6,5,4,3,2,1,0:T(8,128)(2,1)S(1)} collective-permute-done((bf16[2,2,1,1,1,32,768]{6,5,4,3,2,1,0:T(8,128)(2,1)S(1)}, bf16[2,2,1,1,1,32,768]{6,5,4,3,2,1,0:T(8,128)(2,1)S(1)}, u32[]{:S(2)}, u32[]{:S(2)}) %collective-permute-start.21) | collective-permute-done | bytes 196640 | tf_op jit(solution)/shard_map/ppermute | solution.py:150
  (163 shorter events, 93.1 us)
Async XLA Ops:
  0.7 24.7 %collective-permute-start = (bf16[2,1024,128]{2,1,0:T(8,128)(2,1)}, bf16[2,1024,128]{2,1,0:T(8,128)(2,1)}, u32[]{:S(2)}, u32[]{:S(2)}) collective-permute-start(bf16[2,1024,128]{2,1,0:T(8,128)(2,1)} %param.13), channel_id=1, source_target_pairs={{0,8},{4,12},{8,16},{12,20},{16,24},{20,28},{24,0},{28,4},{1,9},{5... | collective-permute-start | bytes 1572872 | tf_op jit(solution)/shard_map/ppermute | solution.py:181
  3.7 25.5 %collective-permute-start.1 = (bf16[2,128,1024]{2,1,0:T(8,128)(2,1)}, bf16[2,128,1024]{2,1,0:T(8,128)(2,1)}, u32[]{:S(2)}, u32[]{:S(2)}) collective-permute-start(bf16[2,128,1024]{2,1,0:T(8,128)(2,1)} %param.14), channel_id=1, source_target_pairs={{0,8},{4,12},{8,16},{12,20},{16,24},{20,28},{24,0},{28,4},{1,9},{5... | collective-permute-start | bytes 1572872 | tf_op jit(solution)/shard_map/ppermute | solution.py:181
  9.2 15.1 %all-to-all-start = ((bf16[4,2,48,1024]{3,2,1,0:T(8,128)(2,1)}), bf16[4,2,48,1024]{3,2,1,0:T(8,128)(2,1)S(1)}, u32[]{:S(2)}, u32[]{:S(2)}) async-start(bf16[4,2,48,1024]{3,2,1,0:T(8,128)(2,1)} %bitcast.1), calls=%async_computation | async-start | bytes 1572864 | tf_op jit(solution)/shard_map/all_to_all | solution.py:217
  29.2 15.9 %all-to-all-start.1 = ((bf16[4,2,48,1024]{3,2,1,0:T(8,128)(2,1)}), bf16[4,2,48,1024]{3,2,1,0:T(8,128)(2,1)}, u32[]{:S(2)}, u32[]{:S(2)}) async-start(bf16[4,2,48,1024]{3,2,1,0:T(8,128)(2,1)} %bitcast.4), calls=%async_computation.1 | async-start | bytes 1572864 | tf_op jit(solution)/shard_map/all_to_all | solution.py:217
  33.4 16.9 %collective-permute-start.2 = (bf16[2,1024,128]{2,1,0:T(8,128)(2,1)}, bf16[2,1024,128]{2,1,0:T(8,128)(2,1)}, u32[]{:S(2)}, u32[]{:S(2)}) collective-permute-start(bf16[2,1024,128]{2,1,0:T(8,128)(2,1)} %collective-permute-done), channel_id=1, source_target_pairs={{0,8},{4,12},{8,16},{12,20},{16,24},{20,28},{24,0},{28,4},{1,9},{5... | collective-permute-start | bytes 1572872 | tf_op jit(solution)/shard_map/ppermute | solution.py:181
  33.5 27.6 %collective-permute-start.3 = (bf16[2,128,1024]{2,1,0:T(8,128)(2,1)}, bf16[2,128,1024]{2,1,0:T(8,128)(2,1)}, u32[]{:S(2)}, u32[]{:S(2)}) collective-permute-start(bf16[2,128,1024]{2,1,0:T(8,128)(2,1)} %collective-permute-done.1), channel_id=1, source_target_pairs={{0,8},{4,12},{8,16},{12,20},{16,24},{20,28},{24,0},{28,4},{1,9},{5... | collective-permute-start | bytes 1572872 | tf_op jit(solution)/shard_map/ppermute | solution.py:181
  34.8 32.6 %collective-permute-start.8 = (bf16[2,192,1024]{2,1,0:T(8,128)(2,1)}, bf16[2,192,1024]{2,1,0:T(8,128)(2,1)}, u32[]{:S(2)}, u32[]{:S(2)}) collective-permute-start(bf16[2,192,1024]{2,1,0:T(8,128)(2,1)} %bitcast.7), channel_id=1, source_target_pairs={{0,4},{4,0},{8,12},{12,8},{16,20},{20,16},{24,28},{28,24},{1,5},{5... | collective-permute-start | bytes 2359304 | tf_op jit(solution)/shard_map/ppermute | solution.py:221
  61.1 16.8 %collective-permute-start.5 = (bf16[2,1024,128]{2,1,0:T(8,128)(2,1)}, bf16[2,1024,128]{2,1,0:T(8,128)(2,1)S(1)}, u32[]{:S(2)}, u32[]{:S(2)}) collective-permute-start(bf16[2,1024,128]{2,1,0:T(8,128)(2,1)} %collective-permute-done.2), channel_id=1, source_target_pairs={{0,8},{4,12},{8,16},{12,20},{16,24},{20,28},{24,0},{28,4},{1,9},{5... | collective-permute-start | bytes 1572872 | tf_op jit(solution)/shard_map/ppermute | solution.py:181
  61.1 26.7 %collective-permute-start.6 = (bf16[2,128,1024]{2,1,0:T(8,128)(2,1)}, bf16[2,128,1024]{2,1,0:T(8,128)(2,1)S(1)}, u32[]{:S(2)}, u32[]{:S(2)}) collective-permute-start(bf16[2,128,1024]{2,1,0:T(8,128)(2,1)} %collective-permute-done.3), channel_id=1, source_target_pairs={{0,8},{4,12},{8,16},{12,20},{16,24},{20,28},{24,0},{28,4},{1,9},{5... | collective-permute-start | bytes 1572872 | tf_op jit(solution)/shard_map/ppermute | solution.py:181
  61.1 26.7 %collective-permute-start.4 = (bf16[2,192,1024]{2,1,0:T(8,128)(2,1)S(1)}, bf16[2,192,1024]{2,1,0:T(8,128)(2,1)S(1)}, u32[]{:S(2)}, u32[]{:S(2)}) collective-permute-start(bf16[2,192,1024]{2,1,0:T(8,128)(2,1)S(1)} %bitcast.63), channel_id=1, source_target_pairs={{0,4},{4,0},{8,12},{12,8},{16,20},{20,16},{24,28},{28,24},{1,5},{5... | collective-permute-start | bytes 2359304 | tf_op jit(solution)/shard_map/ppermute | solution.py:221
  92.8 44.7 %collective-permute-start.7 = (bf16[2,192,1024]{2,1,0:T(8,128)(2,1)}, bf16[2,192,1024]{2,1,0:T(8,128)(2,1)}, u32[]{:S(2)}, u32[]{:S(2)}) collective-permute-start(bf16[2,192,1024]{2,1,0:T(8,128)(2,1)} %slice.43), channel_id=1, source_target_pairs={{0,4},{4,0},{8,12},{12,8},{16,20},{20,16},{24,28},{28,24},{1,5},{5... | collective-permute-start | bytes 2359304 | tf_op jit(solution)/shard_map/ppermute | solution.py:224
  95.5 32.6 %collective-permute-start.9 = (bf16[2,192,1024]{2,1,0:T(8,128)(2,1)S(1)}, bf16[2,192,1024]{2,1,0:T(8,128)(2,1)S(1)}, u32[]{:S(2)}, u32[]{:S(2)}) collective-permute-start(bf16[2,192,1024]{2,1,0:T(8,128)(2,1)S(1)} %slice.42), channel_id=1, source_target_pairs={{0,4},{4,0},{8,12},{12,8},{16,20},{20,16},{24,28},{28,24},{1,5},{5... | collective-permute-start | bytes 2359304 | tf_op jit(solution)/shard_map/ppermute | solution.py:224
  99.5 33.3 %collective-permute-start.11 = (bf16[2,128,1024]{2,1,0:T(8,128)(2,1)S(1)}, bf16[2,128,1024]{2,1,0:T(8,128)(2,1)}, u32[]{:S(2)}, u32[]{:S(2)}) collective-permute-start(bf16[2,128,1024]{2,1,0:T(8,128)(2,1)S(1)} %split.50), channel_id=1, source_target_pairs={{0,8},{4,12},{8,16},{12,20},{16,24},{20,28},{24,0},{28,4},{1,9},{5... | collective-permute-start | bytes 1572872 | tf_op jit(solution)/shard_map/ppermute | solution.py:185
  104.0 31.3 %collective-permute-start.10 = (bf16[2,1024,128]{2,1,0:T(8,128)(2,1)}, bf16[2,1024,128]{2,1,0:T(8,128)(2,1)}, u32[]{:S(2)}, u32[]{:S(2)}) collective-permute-start(bf16[2,1024,128]{2,1,0:T(8,128)(2,1)} %split.51), channel_id=1, source_target_pairs={{0,8},{4,12},{8,16},{12,20},{16,24},{20,28},{24,0},{28,4},{1,9},{5... | collective-permute-start | bytes 1572872 | tf_op jit(solution)/shard_map/ppermute | solution.py:185
  129.3 15.1 %all-to-all-start.3 = ((bf16[2,4,48,1024]{3,2,0,1:T(8,128)(2,1)}), bf16[2,4,48,1024]{3,2,0,1:T(8,128)(2,1)S(1)}, u32[]{:S(2)}, u32[]{:S(2)}) async-start(bf16[2,4,48,1024]{3,2,0,1:T(8,128)(2,1)} %copy.30), calls=%async_computation.3 | async-start | bytes 1572864 | tf_op jit(solution)/shard_map/all_to_all | solution.py:227
  144.4 15.9 %all-to-all-start.2 = ((bf16[2,4,48,1024]{3,2,0,1:T(8,128)(2,1)}), bf16[2,4,48,1024]{3,2,0,1:T(8,128)(2,1)}, u32[]{:S(2)}, u32[]{:S(2)}) async-start(bf16[2,4,48,1024]{3,2,0,1:T(8,128)(2,1)} %copy.29), calls=%async_computation.2 | async-start | bytes 1572864 | tf_op jit(solution)/shard_map/all_to_all | solution.py:227
  149.1 16.9 %collective-permute-start.12 = (bf16[2,1024,128]{2,1,0:T(8,128)(2,1)}, bf16[2,1024,128]{2,1,0:T(8,128)(2,1)}, u32[]{:S(2)}, u32[]{:S(2)}) collective-permute-start(bf16[2,1024,128]{2,1,0:T(8,128)(2,1)} %slice_add_fusion.7), channel_id=1, source_target_pairs={{0,8},{4,12},{8,16},{12,20},{16,24},{20,28},{24,0},{28,4},{1,9},{5... | collective-permute-start | bytes 1572872 | tf_op jit(solution)/shard_map/ppermute | solution.py:185
  149.2 27.6 %collective-permute-start.13 = (bf16[2,128,1024]{2,1,0:T(8,128)(2,1)}, bf16[2,128,1024]{2,1,0:T(8,128)(2,1)}, u32[]{:S(2)}, u32[]{:S(2)}) collective-permute-start(bf16[2,128,1024]{2,1,0:T(8,128)(2,1)} %slice_add_fusion.6), channel_id=1, source_target_pairs={{0,8},{4,12},{8,16},{12,20},{16,24},{20,28},{24,0},{28,4},{1,9},{5... | collective-permute-start | bytes 1572872 | tf_op jit(solution)/shard_map/ppermute | solution.py:185
  159.3 20.5 %collective-permute-start.24 = (bf16[2,2,2,2,1,32,512]{6,5,4,3,2,1,0:T(8,128)(2,1)}, bf16[2,2,2,2,1,32,512]{6,5,4,3,2,1,0:T(8,128)(2,1)}, u32[]{:S(2)}, u32[]{:S(2)}) collective-permute-start(bf16[2,2,2,2,1,32,512]{6,5,4,3,2,1,0:T(8,128)(2,1)} %dynamic-slice_convert_fusion.2), channel_id=1, source_target_pairs={{0,1},{1,0},{2,3},{3,2},{4,5},{5,4},{6,7},{7,6},{8,9},{9,8},{10,11... | collective-permute-start | bytes 1572872 | tf_op jit(solution)/shard_map/ppermute | solution.py:150
  178.3 33.5 %collective-permute-start.29 = (bf16[2,1024,128]{2,1,0:T(8,128)(2,1)S(1)}, bf16[2,1024,128]{2,1,0:T(8,128)(2,1)S(1)}, u32[]{:S(2)}, u32[]{:S(2)}) collective-permute-start(bf16[2,1024,128]{2,1,0:T(8,128)(2,1)S(1)} %slice_add_fusion.5), channel_id=1, source_target_pairs={{0,8},{4,12},{8,16},{12,20},{16,24},{20,28},{24,0},{28,4},{1,9},{5... | collective-permute-start | bytes 1572872 | tf_op jit(solution)/shard_map/ppermute | solution.py:185
  178.4 39.2 %collective-permute-start.30 = (bf16[2,128,1024]{2,1,0:T(8,128)(2,1)S(1)}, bf16[2,128,1024]{2,1,0:T(8,128)(2,1)S(1)}, u32[]{:S(2)}, u32[]{:S(2)}) collective-permute-start(bf16[2,128,1024]{2,1,0:T(8,128)(2,1)S(1)} %slice_add_fusion.4), channel_id=1, source_target_pairs={{0,8},{4,12},{8,16},{12,20},{16,24},{20,28},{24,0},{28,4},{1,9},{5... | collective-permute-start | bytes 1572872 | tf_op jit(solution)/shard_map/ppermute | solution.py:185
  183.5 30.7 %collective-permute-start.19 = (bf16[2,2,2,2,1,32,768]{6,5,4,3,2,1,0:T(8,128)(2,1)S(1)}, bf16[2,2,2,2,1,32,768]{6,5,4,3,2,1,0:T(8,128)(2,1)S(1)}, u32[]{:S(2)}, u32[]{:S(2)}) collective-permute-start(bf16[2,2,2,2,1,32,768]{6,5,4,3,2,1,0:T(8,128)(2,1)S(1)} %dynamic-slice_convert_fusion), channel_id=1, source_target_pairs={{0,1},{1,0},{2,3},{3,2},{4,5},{5,4},{6,7},{7,6},{8,9},{9,8},{10,11... | collective-permute-start | bytes 2359304 | tf_op jit(solution)/shard_map/ppermute | solution.py:150
  190.7 25.3 %collective-permute-start.14 = (bf16[2,2,2,2,1,32,768]{6,5,4,3,2,1,0:T(8,128)(2,1)S(1)}, bf16[2,2,2,2,1,32,768]{6,5,4,3,2,1,0:T(8,128)(2,1)S(1)}, u32[]{:S(2)}, u32[]{:S(2)}) collective-permute-start(bf16[2,2,2,2,1,32,768]{6,5,4,3,2,1,0:T(8,128)(2,1)S(1)} %dynamic-slice_convert_fusion.1), channel_id=1, source_target_pairs={{0,1},{1,0},{2,3},{3,2},{4,5},{5,4},{6,7},{7,6},{8,9},{9,8},{10,11... | collective-permute-start | bytes 2359304 | tf_op jit(solution)/shard_map/ppermute | solution.py:150
  194.3 12.0 %collective-permute-start.27 = (bf16[2,1,1,1,1,32,512]{6,5,4,3,2,1,0:T(8,128)(2,1)S(1)}, bf16[2,1,1,1,1,32,512]{6,5,4,3,2,1,0:T(8,128)(2,1)S(1)}, u32[]{:S(2)}, u32[]{:S(2)}) collective-permute-start(bf16[2,1,1,1,1,32,512]{6,5,4,3,2,1,0:T(8,128)(2,1)S(1)} %dynamic-slice_convert_fusion.11), channel_id=1, source_target_pairs={{0,8},{4,12},{8,0},{12,4},{16,24},{20,28},{24,16},{28,20},{1,9},{5... | collective-permute-start | bytes 196616 | tf_op jit(solution)/shard_map/ppermute | solution.py:150
  (28 other events, 157.1 us)

commit v3 on v2

--- a/solution.py
+++ b/solution.py
@@ -78,7 +78,7 @@
     inner_ref[...] = rms_norm(resid.astype(jnp.float32))
 
 
-def back_kernel(grad_ref, col_ref, row_ref, wo_ref, packed_ref, out_ref, mixed_grad_ref):
+def back_kernel(grad_ref, col_ref, row_ref, wo_ref, packed_ref, normed_ref, mixed_ref, out_ref, left_ref, right_ref, mixed_grad_ref):
     width = wo_ref.shape[1]
     first = first_half()
     mixed_grad_ref[...] = jnp.dot(
@@ -108,6 +108,14 @@
                 out_ref[rows, pl.ds(at * width + pair * 128, 128)] = jnp.where(
                     first, left, right
                 ).astype(jnp.bfloat16)
+    add_terms(grad_ref, normed_ref, mixed_ref, out_ref, left_ref, right_ref)
+
+
+def add_terms(grad_ref, normed_ref, mixed_ref, out_ref, left_ref, right_ref):
+    width = mixed_ref.shape[1]
+    left_ref[...] = row_contract(normed_ref[...], out_ref[:, : 2 * width])
+    right_ref[:, :width] = row_contract(normed_ref[...], out_ref[:, 2 * width :])
+    right_ref[:, width:] = row_contract(grad_ref[...], mixed_ref[...])
 
 
 def front(x, col, row, w_qkv, w_o):
@@ -122,15 +130,16 @@
     )(x, col, row, w_qkv, w_o)
 
 
-def attention_back(d_resid, col, row, w_o, packed):
+def attention_back(d_resid, col, row, w_o, packed, normed, mixed):
+    term = jax.ShapeDtypeStruct((normed.shape[1], 2 * mixed.shape[1]), jnp.float32)
     return pl.pallas_call(
         back_kernel,
-        out_shape=jax.ShapeDtypeStruct(packed.shape, jnp.bfloat16),
+        out_shape=[jax.ShapeDtypeStruct(packed.shape, jnp.bfloat16), term, term],
         scratch_shapes=[pltpu.VMEM((packed.shape[0], w_o.shape[1]), jnp.bfloat16)],
-        compiler_params=pltpu.CompilerParams(vmem_limit_bytes=40 * 1024 * 1024),
-        cost_estimate=pl.CostEstimate(flops=6 * 10**9, bytes_accessed=7 * 10**6, transcendentals=0),
+        compiler_params=pltpu.CompilerParams(vmem_limit_bytes=48 * 1024 * 1024),
+        cost_estimate=pl.CostEstimate(flops=6 * 10**9, bytes_accessed=16 * 10**6, transcendentals=0),
         name="attention_back",
-    )(d_resid, col, row, w_o, packed)
+    )(d_resid, col, row, w_o, packed, normed, mixed)
 
 
 def norm_back(values, cotangent):
@@ -151,25 +160,19 @@
     return keep + came.astype(jnp.float32)
 
 
-def scatter_sum(term, late_y):
-    groups, shards = lax.axis_size("dp"), lax.axis_size("expert")
-    rows, cols = term.shape
+def halving_steps(late_y):
     bits = []
-    for name, count in (("dp", groups), ("expert", shards)):
+    for name in ("dp", "expert"):
+        count = lax.axis_size(name)
         bit = count // 2
         while bit:
-            bits.append((name, count, bit))
+            bits.append((name, count, len(bits), bit))
             bit //= 2
-    value = term.reshape((2,) * len(bits) + (rows // (groups * shards), cols))
     expert_bits = [b for b in reversed(bits) if b[0] == "expert"]
     group_bits = [b for b in reversed(bits) if b[0] == "dp"]
     if late_y:
-        order = expert_bits[:1] + group_bits[:1] + expert_bits[1:] + group_bits[1:]
-    else:
-        order = expert_bits + group_bits
-    for one in order:
-        value = halve(value, one[0], one[1], bits.index(one), one[2])
-    return value.reshape(rows // (groups * shards), cols)
+        return expert_bits[:1] + group_bits[:1] + expert_bits[1:] + group_bits[1:]
+    return expert_bits + group_bits
 
 
 def ring_pairs(groups, step):
@@ -179,6 +182,10 @@
 
 def gather_step(slots, pairs):
     return slots + [lax.ppermute(slots[-1], "dp", pairs)]
+
+
+def turned(slots):
+    return slots[:1] + slots[:0:-1]
 
 
 def reduce_step(total, slots, step, pairs):
@@ -199,7 +206,7 @@
     partner = stage_perm(groups, 1)
     forth, back = ring_pairs(groups, 1), ring_pairs(groups, -1)
 
-    ups, downs = gather_step([w_up], forth), gather_step([w_down], forth)
+    ups, downs = gather_step([w_up], forth), gather_step([w_down], back)
 
     ids = expert_of[:, 0]
     at = jnp.arange(tok_rows, dtype=jnp.int32)
@@ -233,14 +240,14 @@
     own_grads = exchange(store)
     normed, packed, mixed, resid, inner = front(layer_in, col, row, w_qkv, w_o)
     store, own_grads, ups, downs = lax.optimization_barrier((to_slots(inner), own_grads, ups, downs))
-    ups, downs = gather_step(ups, forth), gather_step(downs, forth)
+    ups, downs = gather_step(ups, forth), gather_step(downs, back)
     grads_in = with_partner(own_grads)
     own_inputs, ups, downs = lax.optimization_barrier((exchange(store), ups, downs))
     inputs = with_partner(own_inputs)
     while len(ups) < half:
-        ups, downs = gather_step(ups, forth), gather_step(downs, forth)
+        ups, downs = gather_step(ups, forth), gather_step(downs, back)
     full_up = jnp.concatenate(ups, axis=2)
-    full_down = jnp.concatenate(downs, axis=1)
+    full_down = jnp.concatenate(turned(downs), axis=1)
     d_hidden = jnp.einsum("esd,efd->esf", grads_in, full_down, preferred_element_type=jnp.float32)
     pre_act = jnp.einsum("esd,edf->esf", inputs, full_up, preferred_element_type=jnp.float32)
     hidden = gelu_tanh(pre_act).astype(jnp.bfloat16)
@@ -250,31 +257,32 @@
     part_down = jnp.einsum("esf,esd->efd", hidden, grads_in, preferred_element_type=jnp.float32)
     part_up = jnp.einsum("esd,esf->edf", inputs, d_pre, preferred_element_type=jnp.float32)
     slots_up = jnp.split(part_up, half, axis=2)
-    slots_down = jnp.split(part_down, half, axis=1)
+    slots_down = turned(jnp.split(part_down, half, axis=1))
     grad_up = reduce_step(slots_up[1], slots_up, 0, forth)
-    grad_down = reduce_step(slots_down[1], slots_down, 0, forth)
+    grad_down = reduce_step(slots_down[1], slots_down, 0, back)
+    d_inner, hidden, grad_up, grad_down = lax.optimization_barrier((d_inner, hidden, grad_up, grad_down))
+    grad_up = reduce_step(grad_up, slots_up, 1, forth)
+    grad_down = reduce_step(grad_down, slots_down, 1, back)
+    resid_grad = norm_back(resid.astype(jnp.float32), d_inner.astype(jnp.float32))
+    d_resid = (d_out.astype(jnp.float32) + resid_grad).astype(jnp.bfloat16)
+    d_packed, left, right = attention_back(d_resid, col, row, w_o, packed, normed, mixed)
     result = jnp.einsum("esf,efd->esd", hidden, full_down, preferred_element_type=jnp.float32)
     expert_out = to_tokens(result)
     out = (resid.astype(jnp.float32) + expert_out).astype(jnp.bfloat16)
-    d_inner, grad_up, grad_down = lax.optimization_barrier((d_inner, grad_up, grad_down))
-    grad_up = reduce_step(grad_up, slots_up, 1, forth)
-    grad_down = reduce_step(grad_down, slots_down, 1, forth)
-    resid_grad = norm_back(resid.astype(jnp.float32), d_inner.astype(jnp.float32))
-    d_resid = (d_out.astype(jnp.float32) + resid_grad).astype(jnp.bfloat16)
-    grad_o = scatter_sum(row_contract(d_resid, mixed), True)
-    d_packed = attention_back(d_resid, col, row, w_o, packed)
-    d_packed, grad_up, grad_down = lax.optimization_barrier((d_packed, grad_up, grad_down))
-    for step in range(2, half - 1):
-        grad_up = reduce_step(grad_up, slots_up, step, forth)
-        grad_down = reduce_step(grad_down, slots_down, step, forth)
-    split = d_packed.shape[1] // 2
-    grad_qkv = jnp.concatenate(
-        [
-            scatter_sum(row_contract(normed, d_packed[:, :split]), False),
-            scatter_sum(row_contract(normed, d_packed[:, split:]), True),
-        ],
-        axis=1,
-    )
+    left_steps, right_steps = halving_steps(False), halving_steps(True)
+    parts = (2,) * len(left_steps) + (left.shape[0] // (shards * groups), left.shape[1])
+    left, right = left.reshape(parts), right.reshape(parts)
+    for number, (one, other) in enumerate(zip(left_steps, right_steps)):
+        if number == 1:
+            left, right, grad_up, grad_down = lax.optimization_barrier((left, right, grad_up, grad_down))
+            for step in range(2, half - 1):
+                grad_up = reduce_step(grad_up, slots_up, step, forth)
+                grad_down = reduce_step(grad_down, slots_down, step, back)
+        left, right = halve(left, *one), halve(right, *other)
+    left, right = left.reshape(parts[-2:]), right.reshape(parts[-2:])
+    attended = mixed.shape[1]
+    grad_qkv = jnp.concatenate([left, right[:, :attended]], axis=1)
+    grad_o = right[:, attended:]
     d_normed = col_contract(d_packed, w_qkv).astype(jnp.bfloat16)
     input_grad = norm_back(layer_in.astype(jnp.float32), d_normed.astype(jnp.float32))
     grad_input = (d_resid.astype(jnp.float32) + input_grad).astype(jnp.bfloat16)

time: 245 us -> 233 us (0.951)
  waiting for transfers between devices: 131 us -> 87 us
  starting transfers between devices: 37.8 us -> 57.4 us
  other arithmetic: 20.9 us -> 25.4 us
  Pallas kernels: 11.2 us -> 15.3 us
  local copies, waits for them, and re-layouts: 24.3 us -> 27.7 us
    ppermute x15 -> x10, waiting for transfers between devices: 42.4 us -> 11 us  [halve(): came = lax.ppermute(give, axis_name, stage_perm(count, bit))]
    ppermute x2, waiting for transfers between devices: 24.1 us -> 7.86 us  [to_tokens(): lax.ppermute(values[:, received:].astype(jnp.bfloat16), 'dp', partner)]
    ppermute x6, starting transfers between devices: 0.7 us -> 11.9 us  [reduce_step(): came = lax.ppermute(total.astype(jnp.bfloat16), 'dp', pairs)]
    ppermute x6, waiting for transfers between devices: 12.4 us -> 18.9 us  [reduce_step(): came = lax.ppermute(total.astype(jnp.bfloat16), 'dp', pairs)]
    convert_element_type x15 -> x10, local copies, waits for them, and re-layouts: 1.4 us -> 6.57 us  [halve(): lax.dynamic_index_in_dim(values, 1 - own, axis, keepdims=True)]
    add x12 -> x8, other arithmetic: 1.95 us -> 7.12 us  [halve(): return keep + came.astype(jnp.float32)]
    ppermute x6, starting transfers between devices: 5.99 us -> 11.1 us  [gather_step(): return slots + [lax.ppermute(slots[-1], 'dp', pairs)]]
    all_to_all x2, waiting for transfers between devices: 9.4 us -> 4.26 us  [exchange(): lax.all_to_all(store, 'expert', split_axis=0, concat_axis=2, tiled=True)]
  transfers between devices with their start and end apart: 35 -> 30, of which waited for: 24 -> 17; matrix products, arithmetic and copies ran while one was open for 19% -> 23% of each run, Pallas kernels for 5% -> 7%
where the time goes in v3:
time: 233 us; the launch traced here: 232 us
  waiting for transfers between devices  87 us (37%)
  starting transfers between devices  57.4 us (25%)
  local copies, waits for them, and re-layouts  27.7 us (12%)
  other arithmetic  25.4 us (11%)
  matrix products  17.6 us (8%)
  Pallas kernels  15.3 us (7%)
    ppermute x6, waiting for transfers between devices, gather_step(): return slots + [lax.ppermute(slots[-1], 'dp', pairs)]  41 us
    ppermute x6, waiting for transfers between devices, reduce_step(): came = lax.ppermute(total.astype(jnp.bfloat16), 'dp', pairs)  18.9 us
    add x6, other arithmetic, reduce_step(): return came.astype(jnp.float32) + slots[(step + 2) % len(slots)]  13.6 us
    ppermute x10, starting transfers between devices, halve(): came = lax.ppermute(give, axis_name, stage_perm(count, bit))  12.2 us
    ppermute x6, starting transfers between devices, reduce_step(): came = lax.ppermute(total.astype(jnp.bfloat16), 'dp', pairs)  11.9 us
    unnamed x50, local copies, waits for them, and re-layouts  11.4 us
    ppermute x6, starting transfers between devices, gather_step(): return slots + [lax.ppermute(slots[-1], 'dp', pairs)]  11.1 us
    ppermute x10, waiting for transfers between devices, halve(): came = lax.ppermute(give, axis_name, stage_perm(count, bit))  11 us
  transfers between devices with their start and end apart: 30, of which 17 were waited for; matrix products, arithmetic and copies ran while one was open for 23% of the time, Pallas kernels for 7%

profile of v3, /device:TPU:0, one launch (start us, length us, event | category | flops | bytes accessed | tf_op | source)
XLA Modules:
  0.0 231.9 jit_solution(16797765039518935495)
XLA Ops:
  4.6 4.2 %all-to-all-start = ((bf16[4,2,48,1024]{3,2,1,0:T(8,128)(2,1)}), bf16[4,2,48,1024]{3,2,1,0:T(8,128)(2,1)}, u32[]{:S(2)}, u32[]{:S(2)}) async-start(bf16[4,2,48,1024]{3,2,1,0:T(8,128)(2,1)} %bitcast.1), calls=%async_computation | async-start | bytes 1572864 | tf_op jit(solution)/shard_map/all_to_all | solution.py:224
  8.9 3.0 %collective-permute-start = (bf16[2,1024,128]{2,1,0:T(8,128)(2,1)}, bf16[2,1024,128]{2,1,0:T(8,128)(2,1)}, u32[]{:S(2)}, u32[]{:S(2)}) collective-permute-start(bf16[2,1024,128]{2,1,0:T(8,128)(2,1)} %param.13), channel_id=1, source_target_pairs={{0,8},{4,12},{8,16},{12,20},{16,24},{20,28},{24,0},{28,4},{1,9},{5... | collective-permute-start | bytes 1572872 | tf_op jit(solution)/shard_map/ppermute | solution.py:184
  16.1 5.3 %front.1 = (bf16[256,1024]{1,0:T(8,128)(2,1)S(1)}, bf16[256,1536]{1,0:T(8,128)(2,1)S(1)}, bf16[256,512]{1,0:T(8,128)(2,1)S(1)}, bf16[256,1024]{1,0:T(8,128)(2,1)S(1)}, bf16[256,1024]{1,0:T(8,128)(2,1)S(1)}) custom-call(bf16[256,1024]{1,0:T(8,128)(2,1)S(1)} %copy-done, s32[256,1]{1,0:T(8,128)S(1)} %copy.26.col_ref, s32[1,256]{1,0:T(1,128)S(1)} %bitcast.50, ...), custom_call_target="tpu_custom_call" | custom-call | flops 6000000000 | bytes 7000000 | tf_op jit(solution)/shard_map/front/pallas_call | solution.py:124
  27.1 10.4 %collective-permute-done.1 = bf16[2,128,1024]{2,1,0:T(8,128)(2,1)} collective-permute-done((bf16[2,128,1024]{2,1,0:T(8,128)(2,1)}, bf16[2,128,1024]{2,1,0:T(8,128)(2,1)}, u32[]{:S(2)}, u32[]{:S(2)}) %collective-permute-start.1) | collective-permute-done | bytes 524320 | tf_op jit(solution)/shard_map/ppermute | solution.py:184
  37.4 4.2 %all-to-all-start.1 = ((bf16[4,2,48,1024]{3,2,1,0:T(8,128)(2,1)}), bf16[4,2,48,1024]{3,2,1,0:T(8,128)(2,1)}, u32[]{:S(2)}, u32[]{:S(2)}) async-start(bf16[4,2,48,1024]{3,2,1,0:T(8,128)(2,1)} %bitcast.57), calls=%async_computation.1 | async-start | bytes 1572864 | tf_op jit(solution)/shard_map/all_to_all | solution.py:224
  49.1 4.3 %all-to-all-done.1 = bf16[4,2,48,1024]{3,2,1,0:T(8,128)(2,1)} async-done(((bf16[4,2,48,1024]{3,2,1,0:T(8,128)(2,1)}), bf16[4,2,48,1024]{3,2,1,0:T(8,128)(2,1)}, u32[]{:S(2)}, u32[]{:S(2)}) %all-to-all-start.1) | async-done | bytes 786464 | tf_op jit(solution)/shard_map/all_to_all | solution.py:224
  54.6 3.9 %collective-permute-done.3 = bf16[2,1024,128]{2,1,0:T(8,128)(2,1)S(1)} collective-permute-done((bf16[2,1024,128]{2,1,0:T(8,128)(2,1)}, bf16[2,1024,128]{2,1,0:T(8,128)(2,1)S(1)}, u32[]{:S(2)}, u32[]{:S(2)}) %collective-permute-start.3) | collective-permute-done | bytes 524320 | tf_op jit(solution)/shard_map/ppermute | solution.py:184
  58.5 9.8 %collective-permute-done.4 = bf16[2,128,1024]{2,1,0:T(8,128)(2,1)} collective-permute-done((bf16[2,128,1024]{2,1,0:T(8,128)(2,1)}, bf16[2,128,1024]{2,1,0:T(8,128)(2,1)}, u32[]{:S(2)}, u32[]{:S(2)}) %collective-permute-start.4) | collective-permute-done | bytes 524320 | tf_op jit(solution)/shard_map/ppermute | solution.py:184
  76.9 6.3 %collective-permute-done.5 = bf16[2,128,1024]{2,1,0:T(8,128)(2,1)S(1)} collective-permute-done((bf16[2,128,1024]{2,1,0:T(8,128)(2,1)}, bf16[2,128,1024]{2,1,0:T(8,128)(2,1)S(1)}, u32[]{:S(2)}, u32[]{:S(2)}) %collective-permute-start.5) | collective-permute-done | bytes 524320 | tf_op jit(solution)/shard_map/ppermute | solution.py:184
  85.4 8.9 %collective-permute-done.7 = bf16[2,1024,128]{2,1,0:T(8,128)(2,1)S(1)} collective-permute-done((bf16[2,1024,128]{2,1,0:T(8,128)(2,1)S(1)}, bf16[2,1024,128]{2,1,0:T(8,128)(2,1)S(1)}, u32[]{:S(2)}, u32[]{:S(2)}) %collective-permute-start.7) | collective-permute-done | bytes 524320 | tf_op jit(solution)/shard_map/ppermute | solution.py:184
  106.3 2.7 %collective-permute-start.10 = (bf16[2,128,1024]{2,1,0:T(8,128)(2,1)}, bf16[2,128,1024]{2,1,0:T(8,128)(2,1)}, u32[]{:S(2)}, u32[]{:S(2)}) collective-permute-start(bf16[2,128,1024]{2,1,0:T(8,128)(2,1)} %split.50), channel_id=1, source_target_pairs={{0,24},{4,28},{8,0},{12,4},{16,8},{20,12},{24,16},{28,20},{1,25},{... | collective-permute-start | bytes 1572872 | tf_op jit(solution)/shard_map/ppermute | solution.py:192
  109.0 7.9 %collective-permute-done.8 = bf16[2,192,1024]{2,1,0:T(8,128)(2,1)S(1)} collective-permute-done((bf16[2,192,1024]{2,1,0:T(8,128)(2,1)S(1)}, bf16[2,192,1024]{2,1,0:T(8,128)(2,1)S(1)}, u32[]{:S(2)}, u32[]{:S(2)}) %collective-permute-start.8) | collective-permute-done | bytes 786464 | tf_op jit(solution)/shard_map/ppermute | solution.py:231
  118.1 4.2 %all-to-all-start.2 = ((bf16[2,4,48,1024]{3,2,0,1:T(8,128)(2,1)}), bf16[2,4,48,1024]{3,2,0,1:T(8,128)(2,1)}, u32[]{:S(2)}, u32[]{:S(2)}) async-start(bf16[2,4,48,1024]{3,2,0,1:T(8,128)(2,1)} %copy.29), calls=%async_computation.2 | async-start | bytes 1572864 | tf_op jit(solution)/shard_map/all_to_all | solution.py:234
  124.7 3.0 %collective-permute-done.10 = bf16[2,128,1024]{2,1,0:T(8,128)(2,1)} collective-permute-done((bf16[2,128,1024]{2,1,0:T(8,128)(2,1)}, bf16[2,128,1024]{2,1,0:T(8,128)(2,1)}, u32[]{:S(2)}, u32[]{:S(2)}) %collective-permute-start.10) | collective-permute-done | bytes 524320 | tf_op jit(solution)/shard_map/ppermute | solution.py:192
  130.0 4.0 %all-to-all-done.2 = bf16[2,4,48,1024]{3,2,0,1:T(8,128)(2,1)} async-done(((bf16[2,4,48,1024]{3,2,0,1:T(8,128)(2,1)}), bf16[2,4,48,1024]{3,2,0,1:T(8,128)(2,1)}, u32[]{:S(2)}, u32[]{:S(2)}) %all-to-all-start.2) | async-done | bytes 786464 | tf_op jit(solution)/shard_map/all_to_all | solution.py:234
  135.6 2.8 %fusion.30 = f32[2,384,1024]{2,1,0:T(8,128)S(1)} fusion(bf16[2,384,512]{2,1,0:T(8,128)(2,1)} %copy-done.16, bf16[2,512,1024]{2,1,0:T(8,128)(2,1)} %copy-done.11), kind=kOutput, calls=%fused_computation.99 | convolution fusion | flops 805306368 | bytes 6029312 | tf_op jit(solution)/shard_map/esf,efd->esd/dot_general | solution.py:269
  142.2 10.0 %attention_back.1 = (bf16[256,1536]{1,0:T(8,128)(2,1)S(1)}, f32[1024,1024]{1,0:T(8,128)}, f32[1024,1024]{1,0:T(8,128)}) custom-call(bf16[256,1024]{1,0:T(8,128)(2,1)S(1)} %fusion.12.grad_ref, s32[256,1]{1,0:T(8,128)S(1)} %copy.26.col_ref, s32[1,256]{1,0:T(1,128)S(1)} %bitcast.51, bf16[1024,512]{1,0:T(8,128)(2,1)S(1)} %copy-done.4, ...), custom_call_target="tpu_custom_call" | custom-call | flops 6000000000 | bytes 16000000 | tf_op jit(solution)/shard_map/attention_back/pallas_call | solution.py:135
  155.9 2.9 %collective-permute-start.15 = (bf16[2,128,1024]{2,1,0:T(8,128)(2,1)S(1)}, bf16[2,128,1024]{2,1,0:T(8,128)(2,1)S(1)}, u32[]{:S(2)}, u32[]{:S(2)}) collective-permute-start(bf16[2,128,1024]{2,1,0:T(8,128)(2,1)S(1)} %copy-done.20), channel_id=1, source_target_pairs={{0,24},{4,28},{8,0},{12,4},{16,8},{20,12},{24,16},{28,20},{1,25},{... | collective-permute-start | bytes 1572872 | tf_op jit(solution)/shard_map/ppermute | solution.py:192
  158.8 2.7 %dynamic-slice_convert_fusion = bf16[2,2,2,2,1,32,1024]{6,5,4,3,2,1,0:T(8,128)(2,1)} fusion(f32[2,2,2,2,2,32,1024]{6,5,4,3,2,1,0:T(8,128)} %bitcast.60, s32[]{:T(128)S(6)} %select_n.99), kind=kLoop, calls=%fused_computation.3 | loop fusion | bytes 2097156 | tf_op jit(solution)/shard_map/convert_element_type | solution.py:158
  163.8 7.1 %collective-permute-done.15 = bf16[2,128,1024]{2,1,0:T(8,128)(2,1)S(1)} collective-permute-done((bf16[2,128,1024]{2,1,0:T(8,128)(2,1)S(1)}, bf16[2,128,1024]{2,1,0:T(8,128)(2,1)S(1)}, u32[]{:S(2)}, u32[]{:S(2)}) %collective-permute-start.15) | collective-permute-done | bytes 524320 | tf_op jit(solution)/shard_map/ppermute | solution.py:192
  174.4 3.5 %all-to-all-start.3 = ((bf16[2,4,48,1024]{3,2,0,1:T(8,128)(2,1)}), bf16[2,4,48,1024]{3,2,0,1:T(8,128)(2,1)S(1)}, u32[]{:S(2)}, u32[]{:S(2)}) async-start(bf16[2,4,48,1024]{3,2,0,1:T(8,128)(2,1)} %copy.32), calls=%async_computation.3 | async-start | bytes 1572864 | tf_op jit(solution)/shard_map/all_to_all | solution.py:234
  193.6 4.9 %collective-permute-done.20 = bf16[2,2,1,2,1,32,1024]{6,5,4,3,2,1,0:T(8,128)(2,1)} collective-permute-done((bf16[2,2,1,2,1,32,1024]{6,5,4,3,2,1,0:T(8,128)(2,1)}, bf16[2,2,1,2,1,32,1024]{6,5,4,3,2,1,0:T(8,128)(2,1)}, u32[]{:S(2)}, u32[]{:S(2)}) %collective-permute-start.20) | collective-permute-done | bytes 524320 | tf_op jit(solution)/shard_map/ppermute | solution.py:159
  207.6 7.1 %collective-permute-done.25 = bf16[2,128,1024]{2,1,0:T(8,128)(2,1)S(1)} collective-permute-done((bf16[2,128,1024]{2,1,0:T(8,128)(2,1)}, bf16[2,128,1024]{2,1,0:T(8,128)(2,1)S(1)}, u32[]{:S(2)}, u32[]{:S(2)}) %collective-permute-start.25) | collective-permute-done | bytes 524320 | tf_op jit(solution)/shard_map/ppermute | solution.py:192
  219.5 4.0 %collective-permute-done.22 = bf16[2,1,1,1,1,32,1024]{6,5,4,3,2,1,0:T(8,128)(2,1)S(1)} collective-permute-done((bf16[2,1,1,1,1,32,1024]{6,5,4,3,2,1,0:T(8,128)(2,1)S(1)}, bf16[2,1,1,1,1,32,1024]{6,5,4,3,2,1,0:T(8,128)(2,1)S(1)}, u32[]{:S(2)}, u32[]{:S(2)}) %collective-permute-start.22) | collective-permute-done | bytes 131104 | tf_op jit(solution)/shard_map/ppermute | solution.py:159
  (149 shorter events, 103.3 us)
Async XLA Ops:
  4.6 18.7 %all-to-all-start = ((bf16[4,2,48,1024]{3,2,1,0:T(8,128)(2,1)}), bf16[4,2,48,1024]{3,2,1,0:T(8,128)(2,1)}, u32[]{:S(2)}, u32[]{:S(2)}) async-start(bf16[4,2,48,1024]{3,2,1,0:T(8,128)(2,1)} %bitcast.1), calls=%async_computation | async-start | bytes 1572864 | tf_op jit(solution)/shard_map/all_to_all | solution.py:224
  8.9 18.2 %collective-permute-start = (bf16[2,1024,128]{2,1,0:T(8,128)(2,1)}, bf16[2,1024,128]{2,1,0:T(8,128)(2,1)}, u32[]{:S(2)}, u32[]{:S(2)}) collective-permute-start(bf16[2,1024,128]{2,1,0:T(8,128)(2,1)} %param.13), channel_id=1, source_target_pairs={{0,8},{4,12},{8,16},{12,20},{16,24},{20,28},{24,0},{28,4},{1,9},{5... | collective-permute-start | bytes 1572872 | tf_op jit(solution)/shard_map/ppermute | solution.py:184
  11.9 25.5 %collective-permute-start.1 = (bf16[2,128,1024]{2,1,0:T(8,128)(2,1)}, bf16[2,128,1024]{2,1,0:T(8,128)(2,1)}, u32[]{:S(2)}, u32[]{:S(2)}) collective-permute-start(bf16[2,128,1024]{2,1,0:T(8,128)(2,1)} %param.14), channel_id=1, source_target_pairs={{0,24},{4,28},{8,0},{12,4},{16,8},{20,12},{24,16},{28,20},{1,25},{... | collective-permute-start | bytes 1572872 | tf_op jit(solution)/shard_map/ppermute | solution.py:184
  37.4 15.9 %all-to-all-start.1 = ((bf16[4,2,48,1024]{3,2,1,0:T(8,128)(2,1)}), bf16[4,2,48,1024]{3,2,1,0:T(8,128)(2,1)}, u32[]{:S(2)}, u32[]{:S(2)}) async-start(bf16[4,2,48,1024]{3,2,1,0:T(8,128)(2,1)} %bitcast.57), calls=%async_computation.1 | async-start | bytes 1572864 | tf_op jit(solution)/shard_map/all_to_all | solution.py:224
  41.7 16.8 %collective-permute-start.3 = (bf16[2,1024,128]{2,1,0:T(8,128)(2,1)}, bf16[2,1024,128]{2,1,0:T(8,128)(2,1)S(1)}, u32[]{:S(2)}, u32[]{:S(2)}) collective-permute-start(bf16[2,1024,128]{2,1,0:T(8,128)(2,1)} %collective-permute-done), channel_id=1, source_target_pairs={{0,8},{4,12},{8,16},{12,20},{16,24},{20,28},{24,0},{28,4},{1,9},{5... | collective-permute-start | bytes 1572872 | tf_op jit(solution)/shard_map/ppermute | solution.py:184
  42.8 25.5 %collective-permute-start.4 = (bf16[2,128,1024]{2,1,0:T(8,128)(2,1)}, bf16[2,128,1024]{2,1,0:T(8,128)(2,1)}, u32[]{:S(2)}, u32[]{:S(2)}) collective-permute-start(bf16[2,128,1024]{2,1,0:T(8,128)(2,1)} %collective-permute-done.1), channel_id=1, source_target_pairs={{0,24},{4,28},{8,0},{12,4},{16,8},{20,12},{24,16},{28,20},{1,25},{... | collective-permute-start | bytes 1572872 | tf_op jit(solution)/shard_map/ppermute | solution.py:184
  45.5 30.1 %collective-permute-start.2 = (bf16[2,192,1024]{2,1,0:T(8,128)(2,1)}, bf16[2,192,1024]{2,1,0:T(8,128)(2,1)}, u32[]{:S(2)}, u32[]{:S(2)}) collective-permute-start(bf16[2,192,1024]{2,1,0:T(8,128)(2,1)} %bitcast.52), channel_id=1, source_target_pairs={{0,4},{4,0},{8,12},{12,8},{16,20},{20,16},{24,28},{28,24},{1,5},{5... | collective-permute-start | bytes 2359304 | tf_op jit(solution)/shard_map/ppermute | solution.py:228
  70.4 25.0 %collective-permute-start.6 = (bf16[2,192,1024]{2,1,0:T(8,128)(2,1)S(1)}, bf16[2,192,1024]{2,1,0:T(8,128)(2,1)S(1)}, u32[]{:S(2)}, u32[]{:S(2)}) collective-permute-start(bf16[2,192,1024]{2,1,0:T(8,128)(2,1)S(1)} %bitcast.54), channel_id=1, source_target_pairs={{0,4},{4,0},{8,12},{12,8},{16,20},{20,16},{24,28},{28,24},{1,5},{5... | collective-permute-start | bytes 2359304 | tf_op jit(solution)/shard_map/ppermute | solution.py:228
  74.1 20.1 %collective-permute-start.7 = (bf16[2,1024,128]{2,1,0:T(8,128)(2,1)S(1)}, bf16[2,1024,128]{2,1,0:T(8,128)(2,1)S(1)}, u32[]{:S(2)}, u32[]{:S(2)}) collective-permute-start(bf16[2,1024,128]{2,1,0:T(8,128)(2,1)S(1)} %collective-permute-done.3), channel_id=1, source_target_pairs={{0,8},{4,12},{8,16},{12,20},{16,24},{20,28},{24,0},{28,4},{1,9},{5... | collective-permute-start | bytes 1572872 | tf_op jit(solution)/shard_map/ppermute | solution.py:184
  98.6 18.3 %collective-permute-start.8 = (bf16[2,192,1024]{2,1,0:T(8,128)(2,1)S(1)}, bf16[2,192,1024]{2,1,0:T(8,128)(2,1)S(1)}, u32[]{:S(2)}, u32[]{:S(2)}) collective-permute-start(bf16[2,192,1024]{2,1,0:T(8,128)(2,1)S(1)} %slice.41), channel_id=1, source_target_pairs={{0,4},{4,0},{8,12},{12,8},{16,20},{20,16},{24,28},{28,24},{1,5},{5... | collective-permute-start | bytes 2359304 | tf_op jit(solution)/shard_map/ppermute | solution.py:231
  101.6 20.8 %collective-permute-start.9 = (bf16[2,1024,128]{2,1,0:T(8,128)(2,1)S(1)}, bf16[2,1024,128]{2,1,0:T(8,128)(2,1)}, u32[]{:S(2)}, u32[]{:S(2)}) collective-permute-start(bf16[2,1024,128]{2,1,0:T(8,128)(2,1)S(1)} %split.51), channel_id=1, source_target_pairs={{0,8},{4,12},{8,16},{12,20},{16,24},{20,28},{24,0},{28,4},{1,9},{5... | collective-permute-start | bytes 1572872 | tf_op jit(solution)/shard_map/ppermute | solution.py:192
  106.3 21.4 %collective-permute-start.10 = (bf16[2,128,1024]{2,1,0:T(8,128)(2,1)}, bf16[2,128,1024]{2,1,0:T(8,128)(2,1)}, u32[]{:S(2)}, u32[]{:S(2)}) collective-permute-start(bf16[2,128,1024]{2,1,0:T(8,128)(2,1)} %split.50), channel_id=1, source_target_pairs={{0,24},{4,28},{8,0},{12,4},{16,8},{20,12},{24,16},{28,20},{1,25},{... | collective-permute-start | bytes 1572872 | tf_op jit(solution)/shard_map/ppermute | solution.py:192
  118.1 15.9 %all-to-all-start.2 = ((bf16[2,4,48,1024]{3,2,0,1:T(8,128)(2,1)}), bf16[2,4,48,1024]{3,2,0,1:T(8,128)(2,1)}, u32[]{:S(2)}, u32[]{:S(2)}) async-start(bf16[2,4,48,1024]{3,2,0,1:T(8,128)(2,1)} %copy.29), calls=%async_computation.2 | async-start | bytes 1572864 | tf_op jit(solution)/shard_map/all_to_all | solution.py:234
  138.6 34.6 %collective-permute-start.11 = (bf16[2,192,1024]{2,1,0:T(8,128)(2,1)S(1)}, bf16[2,192,1024]{2,1,0:T(8,128)(2,1)S(1)}, u32[]{:S(2)}, u32[]{:S(2)}) collective-permute-start(bf16[2,192,1024]{2,1,0:T(8,128)(2,1)S(1)} %slice.40), channel_id=1, source_target_pairs={{0,4},{4,0},{8,12},{12,8},{16,20},{20,16},{24,28},{28,24},{1,5},{5... | collective-permute-start | bytes 2359304 | tf_op jit(solution)/shard_map/ppermute | solution.py:231
  140.1 21.5 %collective-permute-start.14 = (bf16[2,1024,128]{2,1,0:T(8,128)(2,1)}, bf16[2,1024,128]{2,1,0:T(8,128)(2,1)S(1)}, u32[]{:S(2)}, u32[]{:S(2)}) collective-permute-start(bf16[2,1024,128]{2,1,0:T(8,128)(2,1)} %slice_add_fusion.7), channel_id=1, source_target_pairs={{0,8},{4,12},{8,16},{12,20},{16,24},{20,28},{24,0},{28,4},{1,9},{5... | collective-permute-start | bytes 1572872 | tf_op jit(solution)/shard_map/ppermute | solution.py:192
  155.8 22.1 %collective-permute-start.12 = (bf16[2,2,2,2,1,32,1024]{6,5,4,3,2,1,0:T(8,128)(2,1)S(1)}, bf16[2,2,2,2,1,32,1024]{6,5,4,3,2,1,0:T(8,128)(2,1)}, u32[]{:S(2)}, u32[]{:S(2)}) collective-permute-start(bf16[2,2,2,2,1,32,1024]{6,5,4,3,2,1,0:T(8,128)(2,1)S(1)} %dynamic-slice_convert_fusion.1), channel_id=1, source_target_pairs={{0,1},{1,0},{2,3},{3,2},{4,5},{5,4},{6,7},{7,6},{8,9},{9,8},{10,11... | collective-permute-start | bytes 3145736 | tf_op jit(solution)/shard_map/ppermute | solution.py:159
  155.9 15.1 %collective-permute-start.15 = (bf16[2,128,1024]{2,1,0:T(8,128)(2,1)S(1)}, bf16[2,128,1024]{2,1,0:T(8,128)(2,1)S(1)}, u32[]{:S(2)}, u32[]{:S(2)}) collective-permute-start(bf16[2,128,1024]{2,1,0:T(8,128)(2,1)S(1)} %copy-done.20), channel_id=1, source_target_pairs={{0,24},{4,28},{8,0},{12,4},{16,8},{20,12},{24,16},{28,20},{1,25},{... | collective-permute-start | bytes 1572872 | tf_op jit(solution)/shard_map/ppermute | solution.py:192
  161.5 18.8 %collective-permute-start.13 = (bf16[2,2,2,2,1,32,1024]{6,5,4,3,2,1,0:T(8,128)(2,1)}, bf16[2,2,2,2,1,32,1024]{6,5,4,3,2,1,0:T(8,128)(2,1)}, u32[]{:S(2)}, u32[]{:S(2)}) collective-permute-start(bf16[2,2,2,2,1,32,1024]{6,5,4,3,2,1,0:T(8,128)(2,1)} %dynamic-slice_convert_fusion), channel_id=1, source_target_pairs={{0,1},{1,0},{2,3},{3,2},{4,5},{5,4},{6,7},{7,6},{8,9},{9,8},{10,11... | collective-permute-start | bytes 3145736 | tf_op jit(solution)/shard_map/ppermute | solution.py:159
  174.4 17.9 %all-to-all-start.3 = ((bf16[2,4,48,1024]{3,2,0,1:T(8,128)(2,1)}), bf16[2,4,48,1024]{3,2,0,1:T(8,128)(2,1)S(1)}, u32[]{:S(2)}, u32[]{:S(2)}) async-start(bf16[2,4,48,1024]{3,2,0,1:T(8,128)(2,1)} %copy.32), calls=%async_computation.3 | async-start | bytes 1572864 | tf_op jit(solution)/shard_map/all_to_all | solution.py:234
  186.4 15.4 %collective-permute-start.16 = (bf16[2,2,2,1,1,32,1024]{6,5,4,3,2,1,0:T(8,128)(2,1)}, bf16[2,2,2,1,1,32,1024]{6,5,4,3,2,1,0:T(8,128)(2,1)}, u32[]{:S(2)}, u32[]{:S(2)}) collective-permute-start(bf16[2,2,2,1,1,32,1024]{6,5,4,3,2,1,0:T(8,128)(2,1)} %dynamic-slice_convert_fusion.3), channel_id=1, source_target_pairs={{0,2},{1,3},{2,0},{3,1},{4,6},{5,7},{6,4},{7,5},{8,10},{9,11},{10,... | collective-permute-start | bytes 1572872 | tf_op jit(solution)/shard_map/ppermute | solution.py:159
  188.4 16.9 %collective-permute-start.24 = (bf16[2,1024,128]{2,1,0:T(8,128)(2,1)}, bf16[2,1024,128]{2,1,0:T(8,128)(2,1)S(1)}, u32[]{:S(2)}, u32[]{:S(2)}) collective-permute-start(bf16[2,1024,128]{2,1,0:T(8,128)(2,1)} %slice_add_fusion.5), channel_id=1, source_target_pairs={{0,8},{4,12},{8,16},{12,20},{16,24},{20,28},{24,0},{28,4},{1,9},{5... | collective-permute-start | bytes 1572872 | tf_op jit(solution)/shard_map/ppermute | solution.py:192
  190.1 24.6 %collective-permute-start.25 = (bf16[2,128,1024]{2,1,0:T(8,128)(2,1)}, bf16[2,128,1024]{2,1,0:T(8,128)(2,1)S(1)}, u32[]{:S(2)}, u32[]{:S(2)}) collective-permute-start(bf16[2,128,1024]{2,1,0:T(8,128)(2,1)} %slice_add_fusion.4), channel_id=1, source_target_pairs={{0,24},{4,28},{8,0},{12,4},{16,8},{20,12},{24,16},{28,20},{1,25},{... | collective-permute-start | bytes 1572872 | tf_op jit(solution)/shard_map/ppermute | solution.py:192
  200.1 17.0 %collective-permute-start.21 = (bf16[2,2,1,1,1,32,1024]{6,5,4,3,2,1,0:T(8,128)(2,1)S(1)}, bf16[2,2,1,1,1,32,1024]{6,5,4,3,2,1,0:T(8,128)(2,1)S(1)}, u32[]{:S(2)}, u32[]{:S(2)}) collective-permute-start(bf16[2,2,1,1,1,32,1024]{6,5,4,3,2,1,0:T(8,128)(2,1)S(1)} %dynamic-slice_convert_fusion.4), channel_id=1, source_target_pairs={{0,2},{1,3},{2,0},{3,1},{4,6},{5,7},{6,4},{7,5},{8,10},{9,11},{10,... | collective-permute-start | bytes 786440 | tf_op jit(solution)/shard_map/ppermute | solution.py:159
  203.0 15.5 %collective-permute-start.17 = (bf16[2,2,1,1,1,32,1024]{6,5,4,3,2,1,0:T(8,128)(2,1)S(1)}, bf16[2,2,1,1,1,32,1024]{6,5,4,3,2,1,0:T(8,128)(2,1)S(1)}, u32[]{:S(2)}, u32[]{:S(2)}) collective-permute-start(bf16[2,2,1,1,1,32,1024]{6,5,4,3,2,1,0:T(8,128)(2,1)S(1)} %dynamic-slice_convert_fusion.5), channel_id=1, source_target_pairs={{0,4},{4,0},{8,12},{12,8},{16,20},{20,16},{24,28},{28,24},{1,5},{5... | collective-permute-start | bytes 786440 | tf_op jit(solution)/shard_map/ppermute | solution.py:159
  (27 other events, 182.0 us)

commit v4 on v3

--- a/solution.py
+++ b/solution.py
@@ -239,11 +239,11 @@
     store, layer_in = lax.optimization_barrier((to_slots(d_out), layer_in))
     own_grads = exchange(store)
     normed, packed, mixed, resid, inner = front(layer_in, col, row, w_qkv, w_o)
-    store, own_grads, ups, downs = lax.optimization_barrier((to_slots(inner), own_grads, ups, downs))
+    own_inputs = exchange(to_slots(inner))
+    own_inputs, own_grads, ups, downs = lax.optimization_barrier((own_inputs, own_grads, ups, downs))
     ups, downs = gather_step(ups, forth), gather_step(downs, back)
-    grads_in = with_partner(own_grads)
-    own_inputs, ups, downs = lax.optimization_barrier((exchange(store), ups, downs))
-    inputs = with_partner(own_inputs)
+    inputs, grads_in = with_partner(own_inputs), with_partner(own_grads)
+    inputs, ups, downs = lax.optimization_barrier((inputs, ups, downs))
     while len(ups) < half:
         ups, downs = gather_step(ups, forth), gather_step(downs, back)
     full_up = jnp.concatenate(ups, axis=2)

time: 233 us -> 241 us (1.034)
  waiting for transfers between devices: 87 us -> 104 us
  local copies, waits for them, and re-layouts: 27.7 us -> 21.9 us
  starting transfers between devices: 57.4 us -> 54.8 us
    ppermute x2, waiting for transfers between devices: 0.01 us -> 19.4 us  [with_partner(): return jnp.concatenate([own, lax.ppermute(own, 'dp', partner)], axis=1)]
    unnamed x50 -> x53, local copies, waits for them, and re-layouts: 11.4 us -> 6.81 us
    all_to_all x2, waiting for transfers between devices: 4.26 us -> 8.05 us  [exchange(): lax.all_to_all(store, 'expert', split_axis=0, concat_axis=2, tiled=True)]
    ppermute x6, waiting for transfers between devices: 41 us -> 37.8 us  [gather_step(): return slots + [lax.ppermute(slots[-1], 'dp', pairs)]]
    ppermute x2, waiting for transfers between devices: 7.86 us -> 5.15 us  [to_tokens(): lax.ppermute(values[:, received:].astype(jnp.bfloat16), 'dp', partner)]
  transfers between devices with their start and end apart: 30 -> 30, of which waited for: 17 -> 17; matrix products, arithmetic and copies ran while one was open for 23% -> 20% of each run, Pallas kernels for 7% -> 6%
where the time goes in v4:
time: 241 us; the launch traced here: 240 us
  waiting for transfers between devices  104 us (43%)
  starting transfers between devices  54.8 us (23%)
  other arithmetic  25.6 us (11%)
  local copies, waits for them, and re-layouts  21.9 us (9%)
  matrix products  17.7 us (7%)
  Pallas kernels  15.4 us (6%)
    ppermute x6, waiting for transfers between devices, gather_step(): return slots + [lax.ppermute(slots[-1], 'dp', pairs)]  37.8 us
    ppermute x2, waiting for transfers between devices, with_partner(): return jnp.concatenate([own, lax.ppermute(own, 'dp', partner)], axis=1)  19.4 us
    ppermute x6, waiting for transfers between devices, reduce_step(): came = lax.ppermute(total.astype(jnp.bfloat16), 'dp', pairs)  17.6 us
    ppermute x10, starting transfers between devices, halve(): came = lax.ppermute(give, axis_name, stage_perm(count, bit))  13.7 us
    add x6, other arithmetic, reduce_step(): return came.astype(jnp.float32) + slots[(step + 2) % len(slots)]  13.6 us
    ppermute x6, starting transfers between devices, reduce_step(): came = lax.ppermute(total.astype(jnp.bfloat16), 'dp', pairs)  11.1 us
    ppermute x6, starting transfers between devices, gather_step(): return slots + [lax.ppermute(slots[-1], 'dp', pairs)]  10.5 us
    ppermute x10, waiting for transfers between devices, halve(): came = lax.ppermute(give, axis_name, stage_perm(count, bit))  10.2 us
  transfers between devices with their start and end apart: 30, of which 17 were waited for; matrix products, arithmetic and copies ran while one was open for 20% of the time, Pallas kernels for 6%

profile of v4, /device:TPU:0, one launch (start us, length us, event | category | flops | bytes accessed | tf_op | source)
XLA Modules:
  0.0 240.3 jit_solution(10655014057041064473)
XLA Ops:
  4.6 4.2 %all-to-all-start.1 = ((bf16[4,2,48,1024]{3,2,1,0:T(8,128)(2,1)}), bf16[4,2,48,1024]{3,2,1,0:T(8,128)(2,1)}, u32[]{:S(2)}, u32[]{:S(2)}) async-start(bf16[4,2,48,1024]{3,2,1,0:T(8,128)(2,1)} %bitcast.1), calls=%async_computation.1 | async-start | bytes 1572864 | tf_op jit(solution)/shard_map/all_to_all | solution.py:224
  10.9 5.3 %front.1 = (bf16[256,1024]{1,0:T(8,128)(2,1)S(1)}, bf16[256,1536]{1,0:T(8,128)(2,1)S(1)}, bf16[256,512]{1,0:T(8,128)(2,1)S(1)}, bf16[256,1024]{1,0:T(8,128)(2,1)S(1)}, bf16[256,1024]{1,0:T(8,128)(2,1)S(1)}) custom-call(bf16[256,1024]{1,0:T(8,128)(2,1)S(1)} %copy-done, s32[256,1]{1,0:T(8,128)S(1)} %copy.34.col_ref, s32[1,256]{1,0:T(1,128)S(1)} %bitcast.51, ...), custom_call_target="tpu_custom_call" | custom-call | flops 6000000000 | bytes 7000000 | tf_op jit(solution)/shard_map/front/pallas_call | solution.py:124
  18.2 3.0 %all-to-all-done.1 = bf16[4,2,48,1024]{3,2,1,0:T(8,128)(2,1)} async-done(((bf16[4,2,48,1024]{3,2,1,0:T(8,128)(2,1)}), bf16[4,2,48,1024]{3,2,1,0:T(8,128)(2,1)}, u32[]{:S(2)}, u32[]{:S(2)}) %all-to-all-start.1) | async-done | bytes 786464 | tf_op jit(solution)/shard_map/all_to_all | solution.py:224
  21.2 4.2 %all-to-all-start = ((bf16[4,2,48,1024]{3,2,1,0:T(8,128)(2,1)}), bf16[4,2,48,1024]{3,2,1,0:T(8,128)(2,1)}, u32[]{:S(2)}, u32[]{:S(2)}) async-start(bf16[4,2,48,1024]{3,2,1,0:T(8,128)(2,1)} %bitcast.56), calls=%async_computation | async-start | bytes 1572864 | tf_op jit(solution)/shard_map/all_to_all | solution.py:224
  32.0 5.1 %all-to-all-done = bf16[4,2,48,1024]{3,2,1,0:T(8,128)(2,1)} async-done(((bf16[4,2,48,1024]{3,2,1,0:T(8,128)(2,1)}), bf16[4,2,48,1024]{3,2,1,0:T(8,128)(2,1)}, u32[]{:S(2)}, u32[]{:S(2)}) %all-to-all-start) | async-done | bytes 786464 | tf_op jit(solution)/shard_map/all_to_all | solution.py:224
  38.4 4.7 %collective-permute-done = bf16[2,1024,128]{2,1,0:T(8,128)(2,1)} collective-permute-done((bf16[2,1024,128]{2,1,0:T(8,128)(2,1)}, bf16[2,1024,128]{2,1,0:T(8,128)(2,1)}, u32[]{:S(2)}, u32[]{:S(2)}) %collective-permute-start) | collective-permute-done | bytes 524320 | tf_op jit(solution)/shard_map/ppermute | solution.py:184
  43.0 10.4 %collective-permute-done.1 = bf16[2,128,1024]{2,1,0:T(8,128)(2,1)} collective-permute-done((bf16[2,128,1024]{2,1,0:T(8,128)(2,1)}, bf16[2,128,1024]{2,1,0:T(8,128)(2,1)}, u32[]{:S(2)}, u32[]{:S(2)}) %collective-permute-start.1) | collective-permute-done | bytes 524320 | tf_op jit(solution)/shard_map/ppermute | solution.py:184
  56.0 2.7 %collective-permute-start.5 = (bf16[2,128,1024]{2,1,0:T(8,128)(2,1)}, bf16[2,128,1024]{2,1,0:T(8,128)(2,1)S(1)}, u32[]{:S(2)}, u32[]{:S(2)}) collective-permute-start(bf16[2,128,1024]{2,1,0:T(8,128)(2,1)} %collective-permute-done.1), channel_id=1, source_target_pairs={{0,24},{4,28},{8,0},{12,4},{16,8},{20,12},{24,16},{28,20},{1,25},{... | collective-permute-start | bytes 1572872 | tf_op jit(solution)/shard_map/ppermute | solution.py:184
  59.3 14.6 %collective-permute-done.3 = bf16[2,192,1024]{2,1,0:T(8,128)(2,1)S(1)} collective-permute-done((bf16[2,192,1024]{2,1,0:T(8,128)(2,1)S(1)}, bf16[2,192,1024]{2,1,0:T(8,128)(2,1)S(1)}, u32[]{:S(2)}, u32[]{:S(2)}) %collective-permute-start.3) | collective-permute-done | bytes 786464 | tf_op jit(solution)/shard_map/ppermute | solution.py:228
  74.0 6.7 %collective-permute-done.5 = bf16[2,128,1024]{2,1,0:T(8,128)(2,1)S(1)} collective-permute-done((bf16[2,128,1024]{2,1,0:T(8,128)(2,1)}, bf16[2,128,1024]{2,1,0:T(8,128)(2,1)S(1)}, u32[]{:S(2)}, u32[]{:S(2)}) %collective-permute-start.5) | collective-permute-done | bytes 524320 | tf_op jit(solution)/shard_map/ppermute | solution.py:184
  84.3 4.9 %collective-permute-done.2 = bf16[2,192,1024]{2,1,0:T(8,128)(2,1)S(1)} collective-permute-done((bf16[2,192,1024]{2,1,0:T(8,128)(2,1)}, bf16[2,192,1024]{2,1,0:T(8,128)(2,1)S(1)}, u32[]{:S(2)}, u32[]{:S(2)}) %collective-permute-start.2) | collective-permute-done | bytes 786464 | tf_op jit(solution)/shard_map/ppermute | solution.py:228
  89.3 16.0 %collective-permute-done.6 = bf16[2,128,1024]{2,1,0:T(8,128)(2,1)S(1)} collective-permute-done((bf16[2,128,1024]{2,1,0:T(8,128)(2,1)S(1)}, bf16[2,128,1024]{2,1,0:T(8,128)(2,1)S(1)}, u32[]{:S(2)}, u32[]{:S(2)}) %collective-permute-start.6) | collective-permute-done | bytes 524320 | tf_op jit(solution)/shard_map/ppermute | solution.py:184
  117.0 3.4 %collective-permute-start.10 = (bf16[2,128,1024]{2,1,0:T(8,128)(2,1)}, bf16[2,128,1024]{2,1,0:T(8,128)(2,1)}, u32[]{:S(2)}, u32[]{:S(2)}) collective-permute-start(bf16[2,128,1024]{2,1,0:T(8,128)(2,1)} %split.50), channel_id=1, source_target_pairs={{0,24},{4,28},{8,0},{12,4},{16,8},{20,12},{24,16},{28,20},{1,25},{... | collective-permute-start | bytes 1572872 | tf_op jit(solution)/shard_map/ppermute | solution.py:192
  120.4 5.1 %collective-permute-done.8 = bf16[2,192,1024]{2,1,0:T(8,128)(2,1)S(1)} collective-permute-done((bf16[2,192,1024]{2,1,0:T(8,128)(2,1)S(1)}, bf16[2,192,1024]{2,1,0:T(8,128)(2,1)S(1)}, u32[]{:S(2)}, u32[]{:S(2)}) %collective-permute-start.8) | collective-permute-done | bytes 786464 | tf_op jit(solution)/shard_map/ppermute | solution.py:231
  126.8 4.2 %all-to-all-start.2 = ((bf16[2,4,48,1024]{3,2,0,1:T(8,128)(2,1)}), bf16[2,4,48,1024]{3,2,0,1:T(8,128)(2,1)}, u32[]{:S(2)}, u32[]{:S(2)}) async-start(bf16[2,4,48,1024]{3,2,0,1:T(8,128)(2,1)} %copy.37), calls=%async_computation.2 | async-start | bytes 1572864 | tf_op jit(solution)/shard_map/all_to_all | solution.py:234
  137.2 5.5 %all-to-all-done.2 = bf16[2,4,48,1024]{3,2,0,1:T(8,128)(2,1)} async-done(((bf16[2,4,48,1024]{3,2,0,1:T(8,128)(2,1)}), bf16[2,4,48,1024]{3,2,0,1:T(8,128)(2,1)}, u32[]{:S(2)}, u32[]{:S(2)}) %all-to-all-start.2) | async-done | bytes 786464 | tf_op jit(solution)/shard_map/all_to_all | solution.py:234
  144.3 2.8 %fusion.30 = f32[2,384,1024]{2,1,0:T(8,128)S(1)} fusion(bf16[2,384,512]{2,1,0:T(8,128)(2,1)} %copy-done.16, bf16[2,512,1024]{2,1,0:T(8,128)(2,1)} %copy-done.11), kind=kOutput, calls=%fused_computation.98 | convolution fusion | flops 805306368 | bytes 6029312 | tf_op jit(solution)/shard_map/esf,efd->esd/dot_general | solution.py:269
  150.6 10.0 %attention_back.1 = (bf16[256,1536]{1,0:T(8,128)(2,1)S(1)}, f32[1024,1024]{1,0:T(8,128)}, f32[1024,1024]{1,0:T(8,128)}) custom-call(bf16[256,1024]{1,0:T(8,128)(2,1)S(1)} %fusion.12.grad_ref, s32[256,1]{1,0:T(8,128)S(1)} %copy.34.col_ref, s32[1,256]{1,0:T(1,128)S(1)} %bitcast.52, bf16[1024,512]{1,0:T(8,128)(2,1)S(1)} %copy-done.4, ...), custom_call_target="tpu_custom_call" | custom-call | flops 6000000000 | bytes 16000000 | tf_op jit(solution)/shard_map/attention_back/pallas_call | solution.py:135
  166.2 2.7 %dynamic-slice_convert_fusion = bf16[2,2,2,2,1,32,1024]{6,5,4,3,2,1,0:T(8,128)(2,1)} fusion(f32[2,2,2,2,2,32,1024]{6,5,4,3,2,1,0:T(8,128)} %bitcast.61, s32[]{:T(128)S(6)} %select_n.99), kind=kLoop, calls=%fused_computation.3 | loop fusion | bytes 2097156 | tf_op jit(solution)/shard_map/convert_element_type | solution.py:158
  171.3 7.4 %collective-permute-done.15 = bf16[2,128,1024]{2,1,0:T(8,128)(2,1)S(1)} collective-permute-done((bf16[2,128,1024]{2,1,0:T(8,128)(2,1)S(1)}, bf16[2,128,1024]{2,1,0:T(8,128)(2,1)S(1)}, u32[]{:S(2)}, u32[]{:S(2)}) %collective-permute-start.15) | collective-permute-done | bytes 524320 | tf_op jit(solution)/shard_map/ppermute | solution.py:192
  182.0 3.5 %all-to-all-start.3 = ((bf16[2,4,48,1024]{3,2,0,1:T(8,128)(2,1)}), bf16[2,4,48,1024]{3,2,0,1:T(8,128)(2,1)S(1)}, u32[]{:S(2)}, u32[]{:S(2)}) async-start(bf16[2,4,48,1024]{3,2,0,1:T(8,128)(2,1)} %copy.40), calls=%async_computation.3 | async-start | bytes 1572864 | tf_op jit(solution)/shard_map/all_to_all | solution.py:234
  202.1 4.0 %collective-permute-done.20 = bf16[2,2,1,2,1,32,1024]{6,5,4,3,2,1,0:T(8,128)(2,1)} collective-permute-done((bf16[2,2,1,2,1,32,1024]{6,5,4,3,2,1,0:T(8,128)(2,1)}, bf16[2,2,1,2,1,32,1024]{6,5,4,3,2,1,0:T(8,128)(2,1)}, u32[]{:S(2)}, u32[]{:S(2)}) %collective-permute-start.20) | collective-permute-done | bytes 524320 | tf_op jit(solution)/shard_map/ppermute | solution.py:159
  216.2 7.1 %collective-permute-done.25 = bf16[2,128,1024]{2,1,0:T(8,128)(2,1)S(1)} collective-permute-done((bf16[2,128,1024]{2,1,0:T(8,128)(2,1)}, bf16[2,128,1024]{2,1,0:T(8,128)(2,1)S(1)}, u32[]{:S(2)}, u32[]{:S(2)}) %collective-permute-start.25) | collective-permute-done | bytes 524320 | tf_op jit(solution)/shard_map/ppermute | solution.py:192
  228.0 4.1 %collective-permute-done.22 = bf16[2,1,1,1,1,32,1024]{6,5,4,3,2,1,0:T(8,128)(2,1)S(1)} collective-permute-done((bf16[2,1,1,1,1,32,1024]{6,5,4,3,2,1,0:T(8,128)(2,1)S(1)}, bf16[2,1,1,1,1,32,1024]{6,5,4,3,2,1,0:T(8,128)(2,1)S(1)}, u32[]{:S(2)}, u32[]{:S(2)}) %collective-permute-start.22) | collective-permute-done | bytes 131104 | tf_op jit(solution)/shard_map/ppermute | solution.py:159
  (152 shorter events, 97.3 us)
Async XLA Ops:
  4.6 16.6 %all-to-all-start.1 = ((bf16[4,2,48,1024]{3,2,1,0:T(8,128)(2,1)}), bf16[4,2,48,1024]{3,2,1,0:T(8,128)(2,1)}, u32[]{:S(2)}, u32[]{:S(2)}) async-start(bf16[4,2,48,1024]{3,2,1,0:T(8,128)(2,1)} %bitcast.1), calls=%async_computation.1 | async-start | bytes 1572864 | tf_op jit(solution)/shard_map/all_to_all | solution.py:224
  21.2 15.9 %all-to-all-start = ((bf16[4,2,48,1024]{3,2,1,0:T(8,128)(2,1)}), bf16[4,2,48,1024]{3,2,1,0:T(8,128)(2,1)}, u32[]{:S(2)}, u32[]{:S(2)}) async-start(bf16[4,2,48,1024]{3,2,1,0:T(8,128)(2,1)} %bitcast.56), calls=%async_computation | async-start | bytes 1572864 | tf_op jit(solution)/shard_map/all_to_all | solution.py:224
  25.4 17.6 %collective-permute-start = (bf16[2,1024,128]{2,1,0:T(8,128)(2,1)}, bf16[2,1024,128]{2,1,0:T(8,128)(2,1)}, u32[]{:S(2)}, u32[]{:S(2)}) collective-permute-start(bf16[2,1024,128]{2,1,0:T(8,128)(2,1)} %param.13), channel_id=1, source_target_pairs={{0,8},{4,12},{8,16},{12,20},{16,24},{20,28},{24,0},{28,4},{1,9},{5... | collective-permute-start | bytes 1572872 | tf_op jit(solution)/shard_map/ppermute | solution.py:184
  27.9 25.5 %collective-permute-start.1 = (bf16[2,128,1024]{2,1,0:T(8,128)(2,1)}, bf16[2,128,1024]{2,1,0:T(8,128)(2,1)}, u32[]{:S(2)}, u32[]{:S(2)}) collective-permute-start(bf16[2,128,1024]{2,1,0:T(8,128)(2,1)} %param.14), channel_id=1, source_target_pairs={{0,24},{4,28},{8,0},{12,4},{16,8},{20,12},{24,16},{28,20},{1,25},{... | collective-permute-start | bytes 1572872 | tf_op jit(solution)/shard_map/ppermute | solution.py:184
  53.4 20.5 %collective-permute-start.3 = (bf16[2,192,1024]{2,1,0:T(8,128)(2,1)S(1)}, bf16[2,192,1024]{2,1,0:T(8,128)(2,1)S(1)}, u32[]{:S(2)}, u32[]{:S(2)}) collective-permute-start(bf16[2,192,1024]{2,1,0:T(8,128)(2,1)S(1)} %bitcast.57), channel_id=1, source_target_pairs={{0,4},{4,0},{8,12},{12,8},{16,20},{20,16},{24,28},{28,24},{1,5},{5... | collective-permute-start | bytes 2359304 | tf_op jit(solution)/shard_map/ppermute | solution.py:228
  54.9 19.1 %collective-permute-start.4 = (bf16[2,1024,128]{2,1,0:T(8,128)(2,1)}, bf16[2,1024,128]{2,1,0:T(8,128)(2,1)S(1)}, u32[]{:S(2)}, u32[]{:S(2)}) collective-permute-start(bf16[2,1024,128]{2,1,0:T(8,128)(2,1)} %collective-permute-done), channel_id=1, source_target_pairs={{0,8},{4,12},{8,16},{12,20},{16,24},{20,28},{24,0},{28,4},{1,9},{5... | collective-permute-start | bytes 1572872 | tf_op jit(solution)/shard_map/ppermute | solution.py:184
  56.0 24.8 %collective-permute-start.5 = (bf16[2,128,1024]{2,1,0:T(8,128)(2,1)}, bf16[2,128,1024]{2,1,0:T(8,128)(2,1)S(1)}, u32[]{:S(2)}, u32[]{:S(2)}) collective-permute-start(bf16[2,128,1024]{2,1,0:T(8,128)(2,1)} %collective-permute-done.1), channel_id=1, source_target_pairs={{0,24},{4,28},{8,0},{12,4},{16,8},{20,12},{24,16},{28,20},{1,25},{... | collective-permute-start | bytes 1572872 | tf_op jit(solution)/shard_map/ppermute | solution.py:184
  58.7 30.5 %collective-permute-start.2 = (bf16[2,192,1024]{2,1,0:T(8,128)(2,1)}, bf16[2,192,1024]{2,1,0:T(8,128)(2,1)S(1)}, u32[]{:S(2)}, u32[]{:S(2)}) collective-permute-start(bf16[2,192,1024]{2,1,0:T(8,128)(2,1)} %bitcast.53), channel_id=1, source_target_pairs={{0,4},{4,0},{8,12},{12,8},{16,20},{20,16},{24,28},{28,24},{1,5},{5... | collective-permute-start | bytes 2359304 | tf_op jit(solution)/shard_map/ppermute | solution.py:228
  80.7 24.5 %collective-permute-start.6 = (bf16[2,128,1024]{2,1,0:T(8,128)(2,1)S(1)}, bf16[2,128,1024]{2,1,0:T(8,128)(2,1)S(1)}, u32[]{:S(2)}, u32[]{:S(2)}) collective-permute-start(bf16[2,128,1024]{2,1,0:T(8,128)(2,1)S(1)} %collective-permute-done.5), channel_id=1, source_target_pairs={{0,24},{4,28},{8,0},{12,4},{16,8},{20,12},{24,16},{28,20},{1,25},{... | collective-permute-start | bytes 1572872 | tf_op jit(solution)/shard_map/ppermute | solution.py:184
  82.9 24.9 %collective-permute-start.7 = (bf16[2,1024,128]{2,1,0:T(8,128)(2,1)S(1)}, bf16[2,1024,128]{2,1,0:T(8,128)(2,1)S(1)}, u32[]{:S(2)}, u32[]{:S(2)}) collective-permute-start(bf16[2,1024,128]{2,1,0:T(8,128)(2,1)S(1)} %collective-permute-done.4), channel_id=1, source_target_pairs={{0,8},{4,12},{8,16},{12,20},{16,24},{20,28},{24,0},{28,4},{1,9},{5... | collective-permute-start | bytes 1572872 | tf_op jit(solution)/shard_map/ppermute | solution.py:184
  111.0 14.6 %collective-permute-start.8 = (bf16[2,192,1024]{2,1,0:T(8,128)(2,1)S(1)}, bf16[2,192,1024]{2,1,0:T(8,128)(2,1)S(1)}, u32[]{:S(2)}, u32[]{:S(2)}) collective-permute-start(bf16[2,192,1024]{2,1,0:T(8,128)(2,1)S(1)} %slice.41), channel_id=1, source_target_pairs={{0,4},{4,0},{8,12},{12,8},{16,20},{20,16},{24,28},{28,24},{1,5},{5... | collective-permute-start | bytes 2359304 | tf_op jit(solution)/shard_map/ppermute | solution.py:231
  113.0 18.0 %collective-permute-start.9 = (bf16[2,1024,128]{2,1,0:T(8,128)(2,1)S(1)}, bf16[2,1024,128]{2,1,0:T(8,128)(2,1)}, u32[]{:S(2)}, u32[]{:S(2)}) collective-permute-start(bf16[2,1024,128]{2,1,0:T(8,128)(2,1)S(1)} %split.51), channel_id=1, source_target_pairs={{0,8},{4,12},{8,16},{12,20},{16,24},{20,28},{24,0},{28,4},{1,9},{5... | collective-permute-start | bytes 1572872 | tf_op jit(solution)/shard_map/ppermute | solution.py:192
  117.0 17.8 %collective-permute-start.10 = (bf16[2,128,1024]{2,1,0:T(8,128)(2,1)}, bf16[2,128,1024]{2,1,0:T(8,128)(2,1)}, u32[]{:S(2)}, u32[]{:S(2)}) collective-permute-start(bf16[2,128,1024]{2,1,0:T(8,128)(2,1)} %split.50), channel_id=1, source_target_pairs={{0,24},{4,28},{8,0},{12,4},{16,8},{20,12},{24,16},{28,20},{1,25},{... | collective-permute-start | bytes 1572872 | tf_op jit(solution)/shard_map/ppermute | solution.py:192
  126.8 15.9 %all-to-all-start.2 = ((bf16[2,4,48,1024]{3,2,0,1:T(8,128)(2,1)}), bf16[2,4,48,1024]{3,2,0,1:T(8,128)(2,1)}, u32[]{:S(2)}, u32[]{:S(2)}) async-start(bf16[2,4,48,1024]{3,2,0,1:T(8,128)(2,1)} %copy.37), calls=%async_computation.2 | async-start | bytes 1572864 | tf_op jit(solution)/shard_map/all_to_all | solution.py:234
  147.3 33.6 %collective-permute-start.11 = (bf16[2,192,1024]{2,1,0:T(8,128)(2,1)S(1)}, bf16[2,192,1024]{2,1,0:T(8,128)(2,1)S(1)}, u32[]{:S(2)}, u32[]{:S(2)}) collective-permute-start(bf16[2,192,1024]{2,1,0:T(8,128)(2,1)S(1)} %slice.40), channel_id=1, source_target_pairs={{0,4},{4,0},{8,12},{12,8},{16,20},{20,16},{24,28},{28,24},{1,5},{5... | collective-permute-start | bytes 2359304 | tf_op jit(solution)/shard_map/ppermute | solution.py:231
  147.9 21.2 %collective-permute-start.14 = (bf16[2,1024,128]{2,1,0:T(8,128)(2,1)}, bf16[2,1024,128]{2,1,0:T(8,128)(2,1)S(1)}, u32[]{:S(2)}, u32[]{:S(2)}) collective-permute-start(bf16[2,1024,128]{2,1,0:T(8,128)(2,1)} %slice_add_fusion.7), channel_id=1, source_target_pairs={{0,8},{4,12},{8,16},{12,20},{16,24},{20,28},{24,0},{28,4},{1,9},{5... | collective-permute-start | bytes 1572872 | tf_op jit(solution)/shard_map/ppermute | solution.py:192
  164.3 21.3 %collective-permute-start.12 = (bf16[2,2,2,2,1,32,1024]{6,5,4,3,2,1,0:T(8,128)(2,1)S(1)}, bf16[2,2,2,2,1,32,1024]{6,5,4,3,2,1,0:T(8,128)(2,1)}, u32[]{:S(2)}, u32[]{:S(2)}) collective-permute-start(bf16[2,2,2,2,1,32,1024]{6,5,4,3,2,1,0:T(8,128)(2,1)S(1)} %dynamic-slice_convert_fusion.1), channel_id=1, source_target_pairs={{0,1},{1,0},{2,3},{3,2},{4,5},{5,4},{6,7},{7,6},{8,9},{9,8},{10,11... | collective-permute-start | bytes 3145736 | tf_op jit(solution)/shard_map/ppermute | solution.py:159
  169.0 19.0 %collective-permute-start.13 = (bf16[2,2,2,2,1,32,1024]{6,5,4,3,2,1,0:T(8,128)(2,1)}, bf16[2,2,2,2,1,32,1024]{6,5,4,3,2,1,0:T(8,128)(2,1)}, u32[]{:S(2)}, u32[]{:S(2)}) collective-permute-start(bf16[2,2,2,2,1,32,1024]{6,5,4,3,2,1,0:T(8,128)(2,1)} %dynamic-slice_convert_fusion), channel_id=1, source_target_pairs={{0,1},{1,0},{2,3},{3,2},{4,5},{5,4},{6,7},{7,6},{8,9},{9,8},{10,11... | collective-permute-start | bytes 3145736 | tf_op jit(solution)/shard_map/ppermute | solution.py:159
  182.0 18.8 %all-to-all-start.3 = ((bf16[2,4,48,1024]{3,2,0,1:T(8,128)(2,1)}), bf16[2,4,48,1024]{3,2,0,1:T(8,128)(2,1)S(1)}, u32[]{:S(2)}, u32[]{:S(2)}) async-start(bf16[2,4,48,1024]{3,2,0,1:T(8,128)(2,1)} %copy.40), calls=%async_computation.3 | async-start | bytes 1572864 | tf_op jit(solution)/shard_map/all_to_all | solution.py:234
  191.5 14.6 %collective-permute-start.20 = (bf16[2,2,1,2,1,32,1024]{6,5,4,3,2,1,0:T(8,128)(2,1)}, bf16[2,2,1,2,1,32,1024]{6,5,4,3,2,1,0:T(8,128)(2,1)}, u32[]{:S(2)}, u32[]{:S(2)}) collective-permute-start(bf16[2,2,1,2,1,32,1024]{6,5,4,3,2,1,0:T(8,128)(2,1)} %dynamic-slice_convert_fusion.2), channel_id=1, source_target_pairs={{0,4},{4,0},{8,12},{12,8},{16,20},{20,16},{24,28},{28,24},{1,5},{5... | collective-permute-start | bytes 1572872 | tf_op jit(solution)/shard_map/ppermute | solution.py:159
  197.0 16.9 %collective-permute-start.24 = (bf16[2,1024,128]{2,1,0:T(8,128)(2,1)}, bf16[2,1024,128]{2,1,0:T(8,128)(2,1)S(1)}, u32[]{:S(2)}, u32[]{:S(2)}) collective-permute-start(bf16[2,1024,128]{2,1,0:T(8,128)(2,1)} %slice_add_fusion.5), channel_id=1, source_target_pairs={{0,8},{4,12},{8,16},{12,20},{16,24},{20,28},{24,0},{28,4},{1,9},{5... | collective-permute-start | bytes 1572872 | tf_op jit(solution)/shard_map/ppermute | solution.py:192
  198.7 24.6 %collective-permute-start.25 = (bf16[2,128,1024]{2,1,0:T(8,128)(2,1)}, bf16[2,128,1024]{2,1,0:T(8,128)(2,1)S(1)}, u32[]{:S(2)}, u32[]{:S(2)}) collective-permute-start(bf16[2,128,1024]{2,1,0:T(8,128)(2,1)} %slice_add_fusion.4), channel_id=1, source_target_pairs={{0,24},{4,28},{8,0},{12,4},{16,8},{20,12},{24,16},{28,20},{1,25},{... | collective-permute-start | bytes 1572872 | tf_op jit(solution)/shard_map/ppermute | solution.py:192
  207.7 18.0 %collective-permute-start.21 = (bf16[2,2,1,1,1,32,1024]{6,5,4,3,2,1,0:T(8,128)(2,1)S(1)}, bf16[2,2,1,1,1,32,1024]{6,5,4,3,2,1,0:T(8,128)(2,1)S(1)}, u32[]{:S(2)}, u32[]{:S(2)}) collective-permute-start(bf16[2,2,1,1,1,32,1024]{6,5,4,3,2,1,0:T(8,128)(2,1)S(1)} %dynamic-slice_convert_fusion.4), channel_id=1, source_target_pairs={{0,2},{1,3},{2,0},{3,1},{4,6},{5,7},{6,4},{7,5},{8,10},{9,11},{10,... | collective-permute-start | bytes 786440 | tf_op jit(solution)/shard_map/ppermute | solution.py:159
  210.7 16.2 %collective-permute-start.17 = (bf16[2,2,1,1,1,32,1024]{6,5,4,3,2,1,0:T(8,128)(2,1)S(1)}, bf16[2,2,1,1,1,32,1024]{6,5,4,3,2,1,0:T(8,128)(2,1)S(1)}, u32[]{:S(2)}, u32[]{:S(2)}) collective-permute-start(bf16[2,2,1,1,1,32,1024]{6,5,4,3,2,1,0:T(8,128)(2,1)S(1)} %dynamic-slice_convert_fusion.5), channel_id=1, source_target_pairs={{0,4},{4,0},{8,12},{12,8},{16,20},{20,16},{24,28},{28,24},{1,5},{5... | collective-permute-start | bytes 786440 | tf_op jit(solution)/shard_map/ppermute | solution.py:159
  (29 other events, 230.2 us)
